TPU v7x, 32 devices: a whole 2x2x4 slice. The times are simulated.
32 devices in a mesh: fsdp: 8 (over z, x), seq: 4 (over y, core).
Axes of the slice: x: 2, y: 2, z: 4, core: 2. Of those that a mesh axis runs over, the one named last changes fastest.
Arguments:
- tokens: bfloat16 [8, 512, 768], P('fsdp', 'seq'), may hold values from -6 to 6
- encoder: bfloat16 [8, 512, 768], P('fsdp'), may hold values from -6 to 6
- dec_segments: int32 [8, 512], P('fsdp'), may hold values from 0 to 2, never falling along the last dimension, each value on 1 to 320 neighbouring positions
- enc_segments: int32 [8, 512], P('fsdp'), may hold values from 0 to 2, never falling along the last dimension, each value on 1 to 320 neighbouring positions
- buckets: int32 [512], replicated, may hold values from 0 to 31, as said below
- self_gain: bfloat16 [768], P(('fsdp', 'seq')), may hold values from 0.5 to 1.5
- self_query: bfloat16 [589824], P(('fsdp', 'seq')), may hold values from -0.0546875 to 0.0546875
- self_key: bfloat16 [589824], P(('fsdp', 'seq')), may hold values from -0.21875 to 0.21875
- self_value: bfloat16 [589824], P(('fsdp', 'seq')), may hold values from -0.21875 to 0.21875
- self_output: bfloat16 [589824], P(('fsdp', 'seq')), may hold values from -0.625 to 0.625
- bias_table: bfloat16 [32, 12], replicated, may hold values from -4 to 4
- cross_gain: bfloat16 [768], P(('fsdp', 'seq')), may hold values from 0.5 to 1.5
- cross_query: bfloat16 [589824], P(('fsdp', 'seq')), may hold values from -0.0546875 to 0.0546875
- cross_key: bfloat16 [589824], P(('fsdp', 'seq')), may hold values from -0.21875 to 0.21875
- cross_value: bfloat16 [589824], P(('fsdp', 'seq')), may hold values from -0.21875 to 0.21875
- cross_output: bfloat16 [589824], P(('fsdp', 'seq')), may hold values from -0.625 to 0.625
- ffn_gain: bfloat16 [768], P(('fsdp', 'seq')), may hold values from 0.5 to 1.5
- ffn_gate: bfloat16 [1572864], P(('fsdp', 'seq')), may hold values from -0.21875 to 0.21875
- ffn_up: bfloat16 [1572864], P(('fsdp', 'seq')), may hold values from -0.21875 to 0.21875
- ffn_down: bfloat16 [1572864], P(('fsdp', 'seq')), may hold values from -0.25 to 0.25
- cotangent: bfloat16 [8, 512, 768], P('fsdp', 'seq'), may hold values from -6 to 6
Outputs:
- output: bfloat16 [8, 512, 768], P('fsdp', 'seq')
- grad_tokens: float32 [8, 512, 768], P('fsdp', 'seq')
- grad_encoder: float32 [8, 512, 768], P('fsdp', 'seq')
- grad_self_gain: float32 [768], P(('fsdp', 'seq'))
- grad_self_query: float32 [589824], P(('fsdp', 'seq'))
- grad_self_key: float32 [589824], P(('fsdp', 'seq'))
- grad_self_value: float32 [589824], P(('fsdp', 'seq'))
- grad_self_output: float32 [589824], P(('fsdp', 'seq'))
- grad_bias_table: float32 [32, 12], replicated
- grad_cross_gain: float32 [768], P(('fsdp', 'seq'))
- grad_cross_query: float32 [589824], P(('fsdp', 'seq'))
- grad_cross_key: float32 [589824], P(('fsdp', 'seq'))
- grad_cross_value: float32 [589824], P(('fsdp', 'seq'))
- grad_cross_output: float32 [589824], P(('fsdp', 'seq'))
- grad_ffn_gain: float32 [768], P(('fsdp', 'seq'))
- grad_ffn_gate: float32 [1572864], P(('fsdp', 'seq'))
- grad_ffn_up: float32 [1572864], P(('fsdp', 'seq'))
- grad_ffn_down: float32 [1572864], P(('fsdp', 'seq'))
Inputs may be any that keep to these rules, and one draw needn't show every extreme that they name: buckets[d] is the bucket of a key d positions before its query; it never falls as d grows, equals d for d below 16, and its last entry is 31. `dec_segments`: along each row the ids never fall; every id 0 to 2 appears; the longest document has 320 positions. `enc_segments`: along each row the ids never fall; every id 0 to 2 appears, so each decoder document has encoder positions in its row; the longest has 320 positions.
All inputs are finite; a program needn't handle non-finite values.
Results may differ from a plain program's by a relative error of at most 0.023.
The roundings to bfloat16 on the way count: a program that leaves them out, or rounds other values in their place, can miss the bound.
Values may be sent and summed in bfloat16 or wider, within the bound.
A program may use at most 256 MiB of HBM per device.

v0:
```python
import jax
import jax.numpy as jnp
from jax import lax
from jax.sharding import PartitionSpec as P

HEADS = 12
HEAD_DIM = 64


epsilon = 1e-06
masked_value = -1e30
highest = lax.Precision.HIGHEST


def matmul(first_op, second_op):
    return jnp.dot(first_op, second_op, preferred_element_type=jnp.float32)


def contract_rows(first_op, second_op):
    return lax.dot_general(
        first_op, second_op, (((0,), (0,)), ((), ())), preferred_element_type=jnp.float32
    )


def times_transposed(first_op, second_op):
    return lax.dot_general(
        first_op, second_op, (((1,), (1,)), ((), ())), preferred_element_type=jnp.float32
    )


def rms_forward(values, gain_vector):
    factor = lax.rsqrt(jnp.mean(values * values, axis=-1, keepdims=True) + epsilon)
    return ((values * factor * gain_vector.astype(jnp.float32)).astype(jnp.bfloat16), factor)


def rms_backward(values, factor, gain_vector, upstream):
    scaled = upstream * gain_vector.astype(jnp.float32)
    inner_mean = jnp.mean(scaled * values, axis=-1, keepdims=True)
    grad_values = factor * scaled - values * (factor * factor * factor) * inner_mean
    grad_gain = jnp.sum(upstream * values * factor, axis=0)
    return (grad_values, grad_gain)


def shape_layer(flat_items, model_width):
    return (
        flat_items[0],
        flat_items[1].reshape(model_width, model_width),
        flat_items[2].reshape(model_width, model_width),
        flat_items[3].reshape(model_width, model_width),
        flat_items[4].reshape(model_width, model_width),
        flat_items[5],
        flat_items[6].reshape(model_width, model_width),
        flat_items[7].reshape(model_width, model_width),
        flat_items[8].reshape(model_width, model_width),
        flat_items[9].reshape(model_width, model_width),
        flat_items[10],
        flat_items[11].reshape(model_width, -1),
        flat_items[12].reshape(model_width, -1),
        flat_items[13].reshape(-1, model_width),
    )


def split_heads(values, row_count):
    return values.reshape(row_count, -1, HEADS, HEAD_DIM)


def score_block(query_heads, key_heads, position_bias, allowed):
    scores = (
        jnp.einsum("rqhd,rkhd->rhqk", query_heads, key_heads, preferred_element_type=jnp.float32)
        + position_bias
    )
    return jnp.where(allowed[:, None], scores, masked_value)


def attend(query_heads, key_heads, value_heads, position_bias, allowed):
    scores = score_block(query_heads, key_heads, position_bias, allowed)
    maximum = jnp.max(scores, axis=-1, keepdims=True)
    log_total = maximum + jnp.log(jnp.sum(jnp.exp(scores - maximum), axis=-1, keepdims=True))
    attn_probs = jnp.exp(scores - log_total).astype(jnp.bfloat16)
    mixed_heads = jnp.einsum(
        "rhqk,rkhd->rqhd", attn_probs, value_heads, preferred_element_type=jnp.float32
    )
    return (mixed_heads.astype(jnp.bfloat16), log_total)


def attend_back(query_heads, key_heads, value_heads, position_bias, allowed, log_total, grad_mixed):
    scores = score_block(query_heads, key_heads, position_bias, allowed)
    attn_probs = jnp.exp(scores - log_total)
    grad_probs = jnp.einsum(
        "rqhd,rkhd->rhqk", grad_mixed, value_heads, preferred_element_type=jnp.float32
    )
    grad_value = jnp.einsum(
        "rhqk,rqhd->rkhd",
        attn_probs.astype(jnp.bfloat16),
        grad_mixed,
        preferred_element_type=jnp.float32,
    )
    row_sums = jnp.sum(attn_probs * grad_probs, axis=-1, keepdims=True)
    grad_scores = attn_probs * (grad_probs - row_sums)
    low_scores = grad_scores.astype(jnp.bfloat16)
    grad_query = jnp.einsum(
        "rhqk,rkhd->rqhd", low_scores, key_heads, preferred_element_type=jnp.float32
    ).astype(jnp.bfloat16)
    grad_key = jnp.einsum(
        "rhqk,rqhd->rkhd", low_scores, query_heads, preferred_element_type=jnp.float32
    )
    return (grad_scores, grad_query, grad_key, grad_value)


def geglu(gate_part, up_part):
    return jax.nn.gelu(gate_part, approximate=True) * up_part


def per_device(
    tokens,
    encoder,
    dec_segments,
    enc_segments,
    buckets,
    self_gain,
    self_query,
    self_key,
    self_value,
    self_output,
    bias_table,
    cross_gain,
    cross_query,
    cross_key,
    cross_value,
    cross_output,
    ffn_gain,
    ffn_gate,
    ffn_up,
    ffn_down,
    cotangent,
):
    row_count, block_len, model_width = tokens.shape
    full_len = dec_segments.shape[1]
    enc_len = encoder.shape[1]
    seq_count = lax.axis_size("seq")
    seq_index = lax.axis_index("seq")
    enc_block = enc_len // seq_count
    inputs_flat = tokens.reshape(row_count * block_len, model_width).astype(jnp.float32)
    query_pos = seq_index * block_len + jnp.arange(block_len, dtype=jnp.int32)
    key_pos = jnp.arange(full_len, dtype=jnp.int32)
    distance = query_pos[:, None] - key_pos[None, :]
    bucket_at = jnp.take(buckets, jnp.clip(distance, 0, full_len - 1))
    bucket_ids = jnp.arange(bias_table.shape[0], dtype=jnp.int32)
    onehot = (bucket_at[:, None, :] == bucket_ids[None, :, None]).astype(jnp.bfloat16)
    position_bias = jnp.einsum(
        "qbk,bh->hqk", onehot, bias_table, preferred_element_type=jnp.float32
    )
    own_segments = lax.dynamic_slice_in_dim(dec_segments, seq_index * block_len, block_len, 1)
    self_allowed = (distance >= 0)[None] & (own_segments[:, :, None] == dec_segments[:, None, :])
    cross_allowed = own_segments[:, :, None] == enc_segments[:, None, :]
    gathered = (
        lax.all_gather(self_gain, ("fsdp", "seq"), axis=0, tiled=True),
        lax.all_gather(self_query, ("fsdp", "seq"), axis=0, tiled=True),
        lax.all_gather(self_key, ("fsdp", "seq"), axis=0, tiled=True),
        lax.all_gather(self_value, ("fsdp", "seq"), axis=0, tiled=True),
        lax.all_gather(self_output, ("fsdp", "seq"), axis=0, tiled=True),
        lax.all_gather(cross_gain, ("fsdp", "seq"), axis=0, tiled=True),
        lax.all_gather(cross_query, ("fsdp", "seq"), axis=0, tiled=True),
        lax.all_gather(cross_key, ("fsdp", "seq"), axis=0, tiled=True),
        lax.all_gather(cross_value, ("fsdp", "seq"), axis=0, tiled=True),
        lax.all_gather(cross_output, ("fsdp", "seq"), axis=0, tiled=True),
        lax.all_gather(ffn_gain, ("fsdp", "seq"), axis=0, tiled=True),
        lax.all_gather(ffn_gate, ("fsdp", "seq"), axis=0, tiled=True),
        lax.all_gather(ffn_up, ("fsdp", "seq"), axis=0, tiled=True),
        lax.all_gather(ffn_down, ("fsdp", "seq"), axis=0, tiled=True),
    )
    shaped = shape_layer(gathered, model_width)
    self_full = shaped[0:5]
    cross_full = shaped[5:10]
    ffn_full = shaped[10:14]
    norm_one, factor_one = rms_forward(inputs_flat, self_full[0])
    query_one = matmul(norm_one, self_full[1]).astype(jnp.bfloat16)
    key_one = (
        matmul(norm_one, self_full[2])
        .astype(jnp.bfloat16)
        .reshape(row_count, block_len, model_width)
    )
    value_one = (
        matmul(norm_one, self_full[3])
        .astype(jnp.bfloat16)
        .reshape(row_count, block_len, model_width)
    )
    key_all, value_all = (
        lax.all_gather(key_one, "seq", axis=1, tiled=True),
        lax.all_gather(value_one, "seq", axis=1, tiled=True),
    )
    query_heads_one = split_heads(query_one, row_count)
    key_heads_one = split_heads(key_all, row_count)
    value_heads_one = split_heads(value_all, row_count)
    mixed_one, lse_one = attend(
        query_heads_one, key_heads_one, value_heads_one, position_bias[None], self_allowed
    )
    mixed_one = mixed_one.reshape(row_count * block_len, model_width)
    hidden_one = inputs_flat + matmul(mixed_one, self_full[4])
    norm_two, factor_two = rms_forward(hidden_one, cross_full[0])
    query_two = matmul(norm_two, cross_full[1]).astype(jnp.bfloat16)
    enc_own = lax.dynamic_slice_in_dim(encoder, seq_index * enc_block, enc_block, 1).reshape(
        row_count * enc_block, model_width
    )
    enc_flat = encoder.reshape(row_count * enc_len, model_width)
    key_two = matmul(enc_flat, cross_full[2]).astype(jnp.bfloat16)
    value_two = matmul(enc_flat, cross_full[3]).astype(jnp.bfloat16)
    query_heads_two = split_heads(query_two, row_count)
    key_heads_two = split_heads(key_two, row_count)
    value_heads_two = split_heads(value_two, row_count)
    mixed_two, lse_two = attend(query_heads_two, key_heads_two, value_heads_two, 0.0, cross_allowed)
    mixed_two = mixed_two.reshape(row_count * block_len, model_width)
    hidden_two = hidden_one + matmul(mixed_two, cross_full[4])
    norm_three, factor_three = rms_forward(hidden_two, ffn_full[0])
    gate_value = matmul(norm_three, ffn_full[1])
    up_value = matmul(norm_three, ffn_full[2])
    activation, geglu_back = jax.vjp(geglu, gate_value, up_value)
    hidden_act = activation.astype(jnp.bfloat16)
    result = hidden_two + matmul(hidden_act, ffn_full[3])
    output = result.astype(jnp.bfloat16).reshape(row_count, block_len, model_width)
    self_back = shaped[0:5]
    cross_back = shaped[5:10]
    ffn_back = shaped[10:14]
    grad_out = cotangent.reshape(row_count * block_len, model_width).astype(jnp.float32)
    low_out = grad_out.astype(jnp.bfloat16)
    grad_down = contract_rows(hidden_act, low_out)
    grad_hidden = times_transposed(low_out, ffn_back[3])
    grad_gate, grad_up = geglu_back(grad_hidden)
    low_gate = grad_gate.astype(jnp.bfloat16)
    low_up = grad_up.astype(jnp.bfloat16)
    grad_gate_weight = contract_rows(norm_three, low_gate)
    grad_up_weight = contract_rows(norm_three, low_up)
    grad_norm_three = times_transposed(low_gate, ffn_back[1]) + times_transposed(
        low_up, ffn_back[2]
    )
    grad_residual_three, grad_gain_three = rms_backward(
        hidden_two, factor_three, ffn_back[0], grad_norm_three
    )
    grad_two = grad_out + grad_residual_three
    low_two = grad_two.astype(jnp.bfloat16)
    grad_cross_out = contract_rows(mixed_two, low_two)
    grad_mixed_two = times_transposed(low_two, cross_back[4]).astype(jnp.bfloat16)
    unused_scores, grad_query_two, grad_key_part_two, grad_value_part_two = attend_back(
        query_heads_two,
        key_heads_two,
        value_heads_two,
        0.0,
        cross_allowed,
        lse_two,
        split_heads(grad_mixed_two, row_count),
    )
    grad_key_two, grad_value_two = (
        lax.psum_scatter(
            grad_key_part_two.reshape(row_count, enc_len, model_width).astype(jnp.bfloat16),
            "seq",
            scatter_dimension=1,
            tiled=True,
        ).astype(jnp.float32),
        lax.psum_scatter(
            grad_value_part_two.reshape(row_count, enc_len, model_width).astype(jnp.bfloat16),
            "seq",
            scatter_dimension=1,
            tiled=True,
        ).astype(jnp.float32),
    )
    low_key_two = grad_key_two.astype(jnp.bfloat16).reshape(row_count * enc_block, model_width)
    low_value_two = grad_value_two.astype(jnp.bfloat16).reshape(row_count * enc_block, model_width)
    grad_cross_key = contract_rows(enc_own, low_key_two)
    grad_cross_value = contract_rows(enc_own, low_value_two)
    grad_encoder = (
        times_transposed(low_key_two, cross_back[2])
        + times_transposed(low_value_two, cross_back[3])
    ).reshape(row_count, enc_block, model_width)
    low_query_two = grad_query_two.reshape(row_count * block_len, model_width)
    grad_cross_query = contract_rows(norm_two, low_query_two)
    grad_norm_two = times_transposed(low_query_two, cross_back[1])
    grad_residual_two, grad_gain_two = rms_backward(
        hidden_one, factor_two, cross_back[0], grad_norm_two
    )
    grad_one = grad_two + grad_residual_two
    low_one = grad_one.astype(jnp.bfloat16)
    grad_self_out = contract_rows(mixed_one, low_one)
    grad_mixed_one = times_transposed(low_one, self_back[4]).astype(jnp.bfloat16)
    grad_scores_one, grad_query_one, grad_key_part_one, grad_value_part_one = attend_back(
        query_heads_one,
        key_heads_one,
        value_heads_one,
        position_bias[None],
        self_allowed,
        lse_one,
        split_heads(grad_mixed_one, row_count),
    )
    grad_table = jnp.einsum(
        "qbk,rhqk->bh", onehot.astype(jnp.float32), grad_scores_one, precision=highest
    )
    grad_key_one, grad_value_one = (
        lax.psum_scatter(
            grad_key_part_one.reshape(row_count, full_len, model_width).astype(jnp.bfloat16),
            "seq",
            scatter_dimension=1,
            tiled=True,
        ).astype(jnp.float32),
        lax.psum_scatter(
            grad_value_part_one.reshape(row_count, full_len, model_width).astype(jnp.bfloat16),
            "seq",
            scatter_dimension=1,
            tiled=True,
        ).astype(jnp.float32),
    )
    low_key_one = grad_key_one.astype(jnp.bfloat16).reshape(row_count * block_len, model_width)
    low_value_one = grad_value_one.astype(jnp.bfloat16).reshape(row_count * block_len, model_width)
    low_query_one = grad_query_one.reshape(row_count * block_len, model_width)
    grad_self_query = contract_rows(norm_one, low_query_one)
    grad_self_key = contract_rows(norm_one, low_key_one)
    grad_self_value = contract_rows(norm_one, low_value_one)
    grad_norm_one = (
        times_transposed(low_query_one, self_back[1])
        + times_transposed(low_key_one, self_back[2])
        + times_transposed(low_value_one, self_back[3])
    )
    grad_residual_one, grad_gain_one = rms_backward(
        inputs_flat, factor_one, self_back[0], grad_norm_one
    )
    grad_tokens = (grad_one + grad_residual_one).reshape(row_count, block_len, model_width)
    summed = (
        lax.psum_scatter(grad_gain_one, ("fsdp", "seq"), scatter_dimension=0, tiled=True),
        lax.psum_scatter(
            grad_self_query.reshape(-1), ("fsdp", "seq"), scatter_dimension=0, tiled=True
        ),
        lax.psum_scatter(
            grad_self_key.reshape(-1), ("fsdp", "seq"), scatter_dimension=0, tiled=True
        ),
        lax.psum_scatter(
            grad_self_value.reshape(-1), ("fsdp", "seq"), scatter_dimension=0, tiled=True
        ),
        lax.psum_scatter(
            grad_self_out.reshape(-1), ("fsdp", "seq"), scatter_dimension=0, tiled=True
        ),
        lax.psum_scatter(grad_gain_two, ("fsdp", "seq"), scatter_dimension=0, tiled=True),
        lax.psum_scatter(
            grad_cross_query.reshape(-1), ("fsdp", "seq"), scatter_dimension=0, tiled=True
        ),
        lax.psum_scatter(
            grad_cross_key.reshape(-1), ("fsdp", "seq"), scatter_dimension=0, tiled=True
        ),
        lax.psum_scatter(
            grad_cross_value.reshape(-1), ("fsdp", "seq"), scatter_dimension=0, tiled=True
        ),
        lax.psum_scatter(
            grad_cross_out.reshape(-1), ("fsdp", "seq"), scatter_dimension=0, tiled=True
        ),
        lax.psum_scatter(grad_gain_three, ("fsdp", "seq"), scatter_dimension=0, tiled=True),
        lax.psum_scatter(
            grad_gate_weight.reshape(-1), ("fsdp", "seq"), scatter_dimension=0, tiled=True
        ),
        lax.psum_scatter(
            grad_up_weight.reshape(-1), ("fsdp", "seq"), scatter_dimension=0, tiled=True
        ),
        lax.psum_scatter(grad_down.reshape(-1), ("fsdp", "seq"), scatter_dimension=0, tiled=True),
    )
    table_grad = lax.psum(grad_table, ("fsdp", "seq"))
    return (
        output,
        grad_tokens,
        grad_encoder,
        summed[0],
        summed[1],
        summed[2],
        summed[3],
        summed[4],
        table_grad,
        summed[5],
        summed[6],
        summed[7],
        summed[8],
        summed[9],
        summed[10],
        summed[11],
        summed[12],
        summed[13],
    )


def solution(mesh):
    in_specs = (
        P("fsdp", "seq", None),
        P("fsdp", None, None),
        P("fsdp", None),
        P("fsdp", None),
        P(),
        P(("fsdp", "seq")),
        P(("fsdp", "seq")),
        P(("fsdp", "seq")),
        P(("fsdp", "seq")),
        P(("fsdp", "seq")),
        P(),
        P(("fsdp", "seq")),
        P(("fsdp", "seq")),
        P(("fsdp", "seq")),
        P(("fsdp", "seq")),
        P(("fsdp", "seq")),
        P(("fsdp", "seq")),
        P(("fsdp", "seq")),
        P(("fsdp", "seq")),
        P(("fsdp", "seq")),
        P("fsdp", "seq", None),
    )
    out_specs = (
        P("fsdp", "seq", None),
        P("fsdp", "seq", None),
        P("fsdp", "seq", None),
        P(("fsdp", "seq")),
        P(("fsdp", "seq")),
        P(("fsdp", "seq")),
        P(("fsdp", "seq")),
        P(("fsdp", "seq")),
        P(),
        P(("fsdp", "seq")),
        P(("fsdp", "seq")),
        P(("fsdp", "seq")),
        P(("fsdp", "seq")),
        P(("fsdp", "seq")),
        P(("fsdp", "seq")),
        P(("fsdp", "seq")),
        P(("fsdp", "seq")),
        P(("fsdp", "seq")),
    )
    return jax.shard_map(
        per_device, mesh=mesh, in_specs=in_specs, out_specs=out_specs, check_vma=False
    )
```

profile of v0, /device:TPU:0, one launch (start us, length us, event | category | flops | bytes accessed | tf_op | source)
XLA Modules:
  0.0 1390.4 jit_solution(2039021706337627497)
XLA Ops:
  18.9 42.4 %all-reduce.19 = (bf16[768]{0:T(1024)(128)(2,1)S(1)}, bf16[768]{0:T(1024)(128)(2,1)S(1)}, bf16[768]{0:T(1024)(128)(2,1)S(1)}) all-reduce(bf16[768]{0:T(1024)(128)(2,1)S(1)} %dynamic-update-slice, bf16[768]{0:T(1024)(128)(2,1)S(1)} %dynamic-update-slice.1, ...), channel_id=1, replica_groups=mesh['fsdp'=8,'seq'=4] {'fsdp','seq'}, use_global_device_ids=true, to_apply=%add | all-reduce | flops 2304 | bytes 9216
  62.1 408.2 %gather_fusion = s32[65536]{0:T(1024)S(1)} fusion(s32[512]{0:T(512)S(1)} %copy-done.1, s32[65536]{0:T(1024)S(1)} %broadcast_clamp_fusion), kind=kCustom, calls=%fused_computation | custom fusion | bytes 786432 | tf_op jit(solution)/shard_map/jit(_take)/gather | solution.py:147
  471.4 3.3 fusion.1
  474.8 5.0 copy.75
  480.1 2.6 reshape.708
  483.7 2.6 reshape.705
  487.5 9.4 all-gather
  498.0 2.6 reshape.710
  501.0 12.3 all-gather.1
  514.5 2.7 reshape.716
  518.9 2.3 copy.76
  521.2 2.6 reshape.720
  526.6 2.4 copy.78
  529.0 2.6 reshape.714
  531.6 3.8 reshape.718
  535.3 2.6 fusion.88
  542.1 2.6 reshape.723
  544.7 1.9 select_reduce_fusion
  549.7 5.8 reshape.724
  555.5 27.2 %all-gather.32.cloned.1.call-done = bf16[1572864]{0:T(1024)(128)(2,1)} async-done(((bf16[49152]{0:T(1024)(128)(2,1)}), bf16[1572864]{0:T(1024)(128)(2,1)}) %all-gather.32.cloned.1.call-update) | async-done | bytes 3145744 | tf_op jit(solution)/shard_map/all_gather | solution.py:169
  582.7 5.8 reshape.725
  588.5 3.7 fusion.90
  593.8 49.7 %all-gather.34.cloned.1.call-done = bf16[1572864]{0:T(1024)(128)(2,1)} async-done(((bf16[49152]{0:T(1024)(128)(2,1)}), bf16[1572864]{0:T(1024)(128)(2,1)}) %all-gather.34.cloned.1.call-update) | async-done | bytes 3145744 | tf_op jit(solution)/shard_map/all_gather | solution.py:170
  643.5 6.8 reshape.726
  650.3 4.9 multiply_convert_fusion.1
  661.9 3.8 convolution_convert_fusion.2
  665.8 3.4 multiply_reduce_fusion.1
  669.2 3.7 copy.88
  674.1 3.5 multiply_convert_fusion
  683.4 3.6 convolution_convert_fusion.4
  687.0 4.8 copy.84
  691.8 2.4 copy.103
  694.3 3.0 fusion.72
  697.3 3.2 reshape.747
  700.5 2.2 convolution_convert_fusion.3
  702.7 3.7 copy.86
  707.4 3.0 fusion.80
  710.5 3.2 reshape.743
  713.7 4.6 multiply_reduce_fusion
  718.6 1.9 fusion.69
  720.5 3.2 reshape.742
  723.7 3.2 subtract_multiply_fusion
  729.8 4.9 copy.82
  734.7 2.4 copy.104
  737.2 2.5 convolution_convert_fusion.6
  739.7 2.0 fusion.83
  741.7 3.3 reshape.739
  745.1 3.7 fusion.61
  748.8 7.0 reshape.750
  756.8 4.2 copy.96
  762.0 4.0 copy.95
  770.9 2.0 fusion.46
  772.9 3.2 reshape.746
  776.1 2.0 fusion.48
  778.1 3.2 reshape.745
  782.9 2.0 fusion.55
  784.9 3.2 reshape.741
  788.2 2.0 fusion.58
  790.2 3.2 reshape.740
  793.5 5.2 copy.81
  799.3 7.0 fusion.10
  808.9 40.9 %all-reduce.17 = (f32[768]{0:T(1024)S(1)}, f32[32,12]{0,1:T(8,128)}, f32[768]{0:T(1024)S(1)}, f32[768]{0:T(1024)S(1)}) all-reduce(f32[768]{0:T(1024)S(1)} %get-tuple-element.22, f32[32,12]{0,1:T(8,128)S(1)} %fusion.10, f32[768]{0:T(1024)S(1)} %copy-done.72, ...), channel_id=8, replica_groups=mesh['fsdp'=8,'seq'=4] {'fsdp','seq'}, use_global_device_ids=true, to_apply=%region_17.18.clone | all-reduce | flops 2688 | bytes 21504
  851.6 1.8 fusion.53
  855.6 511.0 %all-reduce.22.cloned.1.call-done = (f32[589824]{0:T(1024)}, f32[589824]{0:T(1024)}, f32[589824]{0:T(1024)}, f32[589824]{0:T(1024)}, f32[589824]{0:T(1024)}, /*i...) async-done(((f32[589824]{0:T(1024)}, f32[589824]{0:T(1024)}, f32[589824]{0:T(1024)}, ...) | async-done | bytes 37748752
  (301 shorter events, 81.6 us)
Async XLA Ops:
  7.2 510.0 %copy-start = (bf16[1,512,768]{2,1,0:T(8,128)(2,1)S(1)}, bf16[1,512,768]{2,1,0:T(8,128)(2,1)}, u32[]{:S(2)}) copy-start(bf16[1,512,768]{2,1,0:T(8,128)(2,1)} %param.22) | copy-start | bytes 2359300
  7.2 54.9 %copy-start.1 = (s32[512]{0:T(512)S(1)}, s32[512]{0:T(512)}, u32[]{:S(2)}) copy-start(s32[512]{0:T(512)} %param.25) | copy-start | bytes 6148
  7.2 472.8 %all-gather.16.cloned.1.call-start = ((), (), s32[]{:S(2)}) async-start(), calls=%async_computation.5 | async-start | bytes 1216512 | tf_op jit(solution)/shard_map/all_gather | solution.py:158
  7.9 475.7 %all-gather.14.cloned.1.call-start = ((), (), s32[]{:S(2)}) async-start(), calls=%async_computation.4 | async-start | bytes 1216512 | tf_op jit(solution)/shard_map/all_gather | solution.py:160
  8.7 489.3 %all-gather.18.cloned.1.call-start = ((), (), s32[]{:S(2)}) async-start(), calls=%async_computation.6 | async-start | bytes 1216512 | tf_op jit(solution)/shard_map/all_gather | solution.py:159
  9.4 505.0 %all-gather.22.cloned.1.call-start = ((), (), s32[]{:S(2)}) async-start(), calls=%async_computation.8 | async-start | bytes 1216512 | tf_op jit(solution)/shard_map/all_gather | solution.py:165
  10.0 511.2 %all-gather.26.cloned.1.call-start = ((), (), s32[]{:S(2)}) async-start(), calls=%async_computation.10 | async-start | bytes 1216512 | tf_op jit(solution)/shard_map/all_gather | solution.py:164
  10.6 518.4 %all-gather.20.cloned.1.call-start = ((), (), s32[]{:S(2)}) async-start(), calls=%async_computation.7 | async-start | bytes 1216512 | tf_op jit(solution)/shard_map/all_gather | solution.py:161
  11.2 520.4 %all-gather.24.cloned.1.call-start = ((), (), s32[]{:S(2)}) async-start(), calls=%async_computation.9 | async-start | bytes 1216512 | tf_op jit(solution)/shard_map/all_gather | solution.py:163
  11.9 530.2 %all-gather.28.cloned.1.call-start = ((), (), s32[]{:S(2)}) async-start(), calls=%async_computation.11 | async-start | bytes 1216512 | tf_op jit(solution)/shard_map/all_gather | solution.py:166
  12.7 537.1 %all-gather.30.cloned.1.call-start = ((), (), s32[]{:S(2)}) async-start(), calls=%async_computation.12 | async-start | bytes 3244032 | tf_op jit(solution)/shard_map/all_gather | solution.py:168
  13.4 569.3 %all-gather.32.cloned.1.call-start = ((), (), s32[]{:S(2)}) async-start(), calls=%async_computation.13 | async-start | bytes 3244032 | tf_op jit(solution)/shard_map/all_gather | solution.py:169
  14.0 629.6 %all-gather.34.cloned.1.call-start = ((), (), s32[]{:S(2)}) async-start(), calls=%async_computation.14 | async-start | bytes 3244032 | tf_op jit(solution)/shard_map/all_gather | solution.py:170
  14.7 751.3 %reduce-scatter.19.cloned.1.call-start = ((), (), s32[]{:S(2)}) async-start(), calls=%async_computation.18 | async-start | bytes 983040
  16.4 484.2 %copy-start.70 = (f32[128]{0:T(128)}, f32[128]{0:T(128)S(1)}, u32[]{:S(2)}) copy-start(f32[128]{0:T(128)S(1)} %get-tuple-element.46) | copy-start | bytes 1540
  62.1 409.3 %copy-start.78 = (bf16[32,12]{0,1:T(8,128)(2,1)S(1)}, bf16[32,12]{0,1:T(8,128)(2,1)}, u32[]{:S(2)}) copy-start(bf16[32,12]{0,1:T(8,128)(2,1)} %param.31) | copy-start | bytes 2308
  474.8 5.0 copy-start.80
  474.8 5.1 copy-start.79
  474.8 7.9 copy-start.9
  480.0 67.6 %copy-start.37 = (pred[128,512]{1,0:T(8,128)(4,1)}, pred[128,512]{1,0:T(8,128)(4,1)S(1)}, u32[]{:S(2)}) copy-start(pred[128,512]{1,0:T(8,128)(4,1)S(1)} %get-tuple-element.51) | copy-start | bytes 196612
  486.3 14.3 %copy-start.11 = (bf16[768,768]{1,0:T(8,128)(2,1)}, bf16[768,768]{1,0:T(8,128)(2,1)S(1)}, u32[]{:S(2)}) copy-start(bf16[768,768]{1,0:T(8,128)(2,1)S(1)} %reshape.705) | copy-start | bytes 3538948
  500.6 16.6 %copy-start.15 = (bf16[768,768]{1,0:T(8,128)(2,1)}, bf16[768,768]{1,0:T(8,128)(2,1)S(1)}, u32[]{:S(2)}) copy-start(bf16[768,768]{1,0:T(8,128)(2,1)S(1)} %reshape.710) | copy-start | bytes 3538948
  517.2 6.6 copy-start.30
  526.6 8.8 copy-start.24
  526.6 8.8 copy-start.50
  531.5 9.0 copy-start.17
  540.5 4.2 copy-start.45
  541.5 5.2 copy-start.74
  542.1 4.6 copy-start.49
  548.6 6.9 copy-start.62
  549.6 5.9 copy-start.76
  593.8 56.5 %copy-start.63 = (bf16[1,128,768]{2,1,0:T(8,128)(2,1)S(1)}, bf16[1,128,768]{2,1,0:T(8,128)(2,1)}, u32[]{:S(2)}) copy-start(bf16[1,128,768]{2,1,0:T(8,128)(2,1)} %param.41) | copy-start | bytes 589828
  650.3 5.0 copy-start.7
  659.5 6.3 copy-start.28
  660.8 5.0 copy-start.36
  660.8 5.0 copy-start.38
  660.8 5.0 copy-start.67
  674.0 93.6 %reduce-scatter.15.cloned.1.call-start = ((), (), s32[]{:S(2)}) async-start(), calls=%async_computation.16 | async-start | bytes 983040
  674.1 4.2 copy-start.20
  694.2 75.0 %reduce-scatter.17.cloned.1.call-start = ((), (), s32[]{:S(2)}) async-start(), calls=%async_computation.17 | async-start | bytes 983040
  707.4 6.3 copy-start.23
  707.4 6.3 copy-start.52
  713.7 4.9 copy-start.27
  713.7 4.9 copy-start.46
  718.3 63.0 %reduce-scatter.13.cloned.1.call-start = ((), (), s32[]{:S(2)}) async-start(), calls=%async_computation.15 | async-start | bytes 983040
  723.7 4.9 copy-start.51
  729.8 7.3 copy-start.25
  734.7 5.0 copy-start.71
  739.7 5.3 copy-start.47
  745.0 621.6 %all-reduce.22.cloned.1.call-start = ((), (), s32[]{:S(2)}) async-start(), calls=%async_computation.19 | async-start | bytes 75497472
  748.8 7.0 copy-start.44
  767.6 8.5 copy-start.53
  769.2 13.6 copy-start.57
  770.9 5.2 copy-start.55
  782.9 5.3 copy-start.59
  793.4 5.3 copy-start.14
  793.5 5.3 copy-start.48
  793.5 5.8 copy-start.40
  798.7 7.6 copy-start.10
  798.7 7.6 copy-start.34
  807.6 43.9 %copy-start.56 = (bf16[1,128,768]{1,2,0:T(8,128)(2,1)S(1)}, bf16[1,128,768]{1,2,0:T(8,128)(2,1)}, u32[]{:S(2)}) copy-start(bf16[1,128,768]{1,2,0:T(8,128)(2,1)} %copy-done.55) | copy-start | bytes 589828
  807.7 45.8 %copy-start.31 = (bf16[768,768]{1,0:T(8,128)(2,1)S(1)}, bf16[768,768]{1,0:T(8,128)(2,1)}, u32[]{:S(2)}) copy-start(bf16[768,768]{1,0:T(8,128)(2,1)} %copy-done.30) | copy-start | bytes 3538948
  807.7 45.8 %copy-start.54 = (bf16[1,128,768]{1,2,0:T(8,128)(2,1)S(1)}, bf16[1,128,768]{1,2,0:T(8,128)(2,1)}, u32[]{:S(2)}) copy-start(bf16[1,128,768]{1,2,0:T(8,128)(2,1)} %copy-done.53) | copy-start | bytes 589828
  808.2 46.5 %copy-start.82 = (f32[128]{0:T(128)S(1)}, f32[128]{0:T(128)}, u32[]{:S(2)}) copy-start(f32[128]{0:T(128)} %get-tuple-element.45) | copy-start | bytes 1540
  (36 other events, 84.2 us)
Sparse Core Ops, SparseCore 0:
  11.0 56.9 all-gather.15
  70.8 53.1 all-gather.13
  127.0 53.0 all-gather.17
  182.8 53.0 all-gather.21
  238.6 53.0 all-gather.25
  294.5 52.9 all-gather.19
  350.4 53.0 all-gather.23
  406.4 53.0 all-gather.27
  462.4 60.0 all-gather.29
  525.1 57.5 all-gather.31
  585.6 57.8 all-gather.33
  674.1 22.0 reduce-scatter.18
  699.0 23.2 reduce-scatter.14
  724.6 23.2 reduce-scatter.16
  750.5 23.1 reduce-scatter.12
  793.6 573.0 all-reduce.21
where the time goes:
time: 1400 us; the launch traced here: 1390 us
  waiting for transfers between devices  595 us (42%)
  local copies, waits for them, and re-layouts  570 us (41%)
  blocking collectives  105 us (8%)
  matrix products  91 us (6%)
  between operations  15.5 us (1%)
    unnamed x21, waiting for transfers between devices  518 us
    gather x2, local copies, waits for them, and re-layouts, per_device(): bucket_at = jnp.take(buckets, jnp.clip(distance, 0, full_len - 1))  408 us
    unnamed x2, blocking collectives  83.3 us
    unnamed x207, local copies, waits for them, and re-layouts  66.8 us
    all_gather x1, waiting for transfers between devices, per_device(): lax.all_gather(ffn_down, ('fsdp', 'seq'), axis=0, tiled=True)  49.7 us
  transfers between devices with their start and end apart: 16, of which 3 were waited for; matrix products, arithmetic and copies ran while one was open for 44% of the time, Pallas kernels for 0%

commit v1 on v0

--- a/solution.py
+++ b/solution.py
@@ -41,23 +41,35 @@
     return (grad_values, grad_gain)
 
 
-def shape_layer(flat_items, model_width):
-    return (
-        flat_items[0],
-        flat_items[1].reshape(model_width, model_width),
-        flat_items[2].reshape(model_width, model_width),
-        flat_items[3].reshape(model_width, model_width),
-        flat_items[4].reshape(model_width, model_width),
-        flat_items[5],
-        flat_items[6].reshape(model_width, model_width),
-        flat_items[7].reshape(model_width, model_width),
-        flat_items[8].reshape(model_width, model_width),
-        flat_items[9].reshape(model_width, model_width),
-        flat_items[10],
-        flat_items[11].reshape(model_width, -1),
-        flat_items[12].reshape(model_width, -1),
-        flat_items[13].reshape(-1, model_width),
-    )
+def gather_rows(packed):
+    return lax.all_gather(packed, ("fsdp", "seq"), axis=0, tiled=True)
+
+
+def scatter_rows(partial):
+    return lax.psum_scatter(partial, ("fsdp", "seq"), scatter_dimension=0, tiled=True)
+
+
+def scatter_to_owner(partial, row_count, block):
+    count = lax.axis_size("seq")
+    index = lax.axis_index("seq")
+    total = lax.dynamic_slice_in_dim(partial, index * block, block, 1).astype(jnp.float32)
+    for step in range(1, count):
+        target = lax.rem(index + step, count)
+        piece = lax.dynamic_slice_in_dim(partial, target * block, block, 1)
+        pairs = [(source, (source + step) % count) for source in range(count)]
+        total = total + lax.ppermute(piece, "seq", pairs).astype(jnp.float32)
+    return total.astype(jnp.bfloat16)
+
+
+def sum_everywhere(values):
+    for axis in ("seq", "fsdp"):
+        count = lax.axis_size(axis)
+        step = 1
+        while step < count:
+            pairs = [(source, source ^ step) for source in range(count)]
+            values = values + lax.ppermute(values, axis, pairs)
+            step *= 2
+    return values
 
 
 def split_heads(values, row_count):
@@ -144,51 +156,77 @@
     query_pos = seq_index * block_len + jnp.arange(block_len, dtype=jnp.int32)
     key_pos = jnp.arange(full_len, dtype=jnp.int32)
     distance = query_pos[:, None] - key_pos[None, :]
-    bucket_at = jnp.take(buckets, jnp.clip(distance, 0, full_len - 1))
     bucket_ids = jnp.arange(bias_table.shape[0], dtype=jnp.int32)
-    onehot = (bucket_at[:, None, :] == bucket_ids[None, :, None]).astype(jnp.bfloat16)
+    first = jnp.sum((buckets[None, :] < bucket_ids[:, None]).astype(jnp.int32), axis=1)
+    beyond = jnp.sum((buckets[None, :] <= bucket_ids[:, None]).astype(jnp.int32), axis=1)
+    clipped = jnp.clip(distance, 0, full_len - 1)[:, None, :]
+    onehot = (
+        (clipped >= first[None, :, None]) & (clipped < beyond[None, :, None])
+    ).astype(jnp.bfloat16)
     position_bias = jnp.einsum(
         "qbk,bh->hqk", onehot, bias_table, preferred_element_type=jnp.float32
     )
     own_segments = lax.dynamic_slice_in_dim(dec_segments, seq_index * block_len, block_len, 1)
     self_allowed = (distance >= 0)[None] & (own_segments[:, :, None] == dec_segments[:, None, :])
     cross_allowed = own_segments[:, :, None] == enc_segments[:, None, :]
-    gathered = (
-        lax.all_gather(self_gain, ("fsdp", "seq"), axis=0, tiled=True),
-        lax.all_gather(self_query, ("fsdp", "seq"), axis=0, tiled=True),
-        lax.all_gather(self_key, ("fsdp", "seq"), axis=0, tiled=True),
-        lax.all_gather(self_value, ("fsdp", "seq"), axis=0, tiled=True),
-        lax.all_gather(self_output, ("fsdp", "seq"), axis=0, tiled=True),
-        lax.all_gather(cross_gain, ("fsdp", "seq"), axis=0, tiled=True),
-        lax.all_gather(cross_query, ("fsdp", "seq"), axis=0, tiled=True),
-        lax.all_gather(cross_key, ("fsdp", "seq"), axis=0, tiled=True),
-        lax.all_gather(cross_value, ("fsdp", "seq"), axis=0, tiled=True),
-        lax.all_gather(cross_output, ("fsdp", "seq"), axis=0, tiled=True),
-        lax.all_gather(ffn_gain, ("fsdp", "seq"), axis=0, tiled=True),
-        lax.all_gather(ffn_gate, ("fsdp", "seq"), axis=0, tiled=True),
-        lax.all_gather(ffn_up, ("fsdp", "seq"), axis=0, tiled=True),
-        lax.all_gather(ffn_down, ("fsdp", "seq"), axis=0, tiled=True),
-    )
-    shaped = shape_layer(gathered, model_width)
-    self_full = shaped[0:5]
-    cross_full = shaped[5:10]
-    ffn_full = shaped[10:14]
+    own_rows = self_gain.shape[0]
+    gains = jnp.pad(
+        jnp.stack([self_gain, cross_gain, ffn_gain], axis=1), ((0, 0), (0, 125))
+    )
+
+    def rows_of(flat):
+        return flat.reshape(own_rows, -1)
+
+    packed_self = gather_rows(
+        jnp.concatenate(
+            [rows_of(w) for w in (self_query, self_key, self_value, self_output)] + [gains],
+            axis=1,
+        )
+    )
+    packed_rest = gather_rows(
+        jnp.concatenate(
+            [
+                rows_of(w)
+                for w in (
+                    cross_query,
+                    cross_key,
+                    cross_value,
+                    cross_output,
+                    ffn_gate,
+                    ffn_up,
+                )
+            ],
+            axis=1,
+        )
+    )
+    packed_cross = packed_rest[:, : 4 * model_width]
+    packed_in = packed_rest[:, 4 * model_width :]
+    packed_down = gather_rows(ffn_down.reshape(-1, model_width))
+    all_gains = packed_self[:, 4 * model_width :]
+
+    def columns(packed, index):
+        return packed[:, index * model_width : (index + 1) * model_width]
+
+    hidden_width = packed_down.shape[0]
+    self_full = [all_gains[:, 0]] + [columns(packed_self, index) for index in range(4)]
+    cross_full = [all_gains[:, 1]] + [columns(packed_cross, index) for index in range(4)]
+    ffn_full = [
+        all_gains[:, 2],
+        packed_in[:, :hidden_width],
+        packed_in[:, hidden_width:],
+        packed_down,
+    ]
     norm_one, factor_one = rms_forward(inputs_flat, self_full[0])
-    query_one = matmul(norm_one, self_full[1]).astype(jnp.bfloat16)
-    key_one = (
-        matmul(norm_one, self_full[2])
-        .astype(jnp.bfloat16)
-        .reshape(row_count, block_len, model_width)
-    )
-    value_one = (
-        matmul(norm_one, self_full[3])
-        .astype(jnp.bfloat16)
-        .reshape(row_count, block_len, model_width)
-    )
-    key_all, value_all = (
-        lax.all_gather(key_one, "seq", axis=1, tiled=True),
-        lax.all_gather(value_one, "seq", axis=1, tiled=True),
-    )
+    qkv_one = matmul(norm_one, packed_self[:, : 3 * model_width]).astype(jnp.bfloat16)
+    query_one = qkv_one[:, :model_width]
+    pair_all = lax.all_gather(
+        qkv_one[:, model_width:].reshape(row_count, block_len, 2 * model_width),
+        "seq",
+        axis=1,
+        tiled=True,
+    )
+    key_all = pair_all[:, :, :model_width]
+    value_all = pair_all[:, :, model_width:]
     query_heads_one = split_heads(query_one, row_count)
     key_heads_one = split_heads(key_all, row_count)
     value_heads_one = split_heads(value_all, row_count)
@@ -218,9 +256,9 @@
     hidden_act = activation.astype(jnp.bfloat16)
     result = hidden_two + matmul(hidden_act, ffn_full[3])
     output = result.astype(jnp.bfloat16).reshape(row_count, block_len, model_width)
-    self_back = shaped[0:5]
-    cross_back = shaped[5:10]
-    ffn_back = shaped[10:14]
+    self_back = self_full
+    cross_back = cross_full
+    ffn_back = ffn_full
     grad_out = cotangent.reshape(row_count * block_len, model_width).astype(jnp.float32)
     low_out = grad_out.astype(jnp.bfloat16)
     grad_down = contract_rows(hidden_act, low_out)
@@ -228,11 +266,10 @@
     grad_gate, grad_up = geglu_back(grad_hidden)
     low_gate = grad_gate.astype(jnp.bfloat16)
     low_up = grad_up.astype(jnp.bfloat16)
-    grad_gate_weight = contract_rows(norm_three, low_gate)
-    grad_up_weight = contract_rows(norm_three, low_up)
-    grad_norm_three = times_transposed(low_gate, ffn_back[1]) + times_transposed(
-        low_up, ffn_back[2]
-    )
+    low_in = jnp.concatenate([low_gate, low_up], axis=1)
+    summed_in = scatter_rows(contract_rows(norm_three, low_in).astype(jnp.bfloat16))
+    summed_down = scatter_rows(grad_down.astype(jnp.bfloat16))
+    grad_norm_three = times_transposed(low_in, packed_in)
     grad_residual_three, grad_gain_three = rms_backward(
         hidden_two, factor_three, ffn_back[0], grad_norm_three
     )
@@ -249,31 +286,28 @@
         lse_two,
         split_heads(grad_mixed_two, row_count),
     )
-    grad_key_two, grad_value_two = (
-        lax.psum_scatter(
-            grad_key_part_two.reshape(row_count, enc_len, model_width).astype(jnp.bfloat16),
-            "seq",
-            scatter_dimension=1,
-            tiled=True,
-        ).astype(jnp.float32),
-        lax.psum_scatter(
-            grad_value_part_two.reshape(row_count, enc_len, model_width).astype(jnp.bfloat16),
-            "seq",
-            scatter_dimension=1,
-            tiled=True,
-        ).astype(jnp.float32),
-    )
-    low_key_two = grad_key_two.astype(jnp.bfloat16).reshape(row_count * enc_block, model_width)
-    low_value_two = grad_value_two.astype(jnp.bfloat16).reshape(row_count * enc_block, model_width)
-    grad_cross_key = contract_rows(enc_own, low_key_two)
-    grad_cross_value = contract_rows(enc_own, low_value_two)
-    grad_encoder = (
-        times_transposed(low_key_two, cross_back[2])
-        + times_transposed(low_value_two, cross_back[3])
+    pair_two = jnp.concatenate(
+        [
+            grad_key_part_two.reshape(row_count, enc_len, model_width),
+            grad_value_part_two.reshape(row_count, enc_len, model_width),
+        ],
+        axis=2,
+    ).astype(jnp.bfloat16)
+    low_pair_two = scatter_to_owner(pair_two, row_count, enc_block).reshape(
+        row_count * enc_block, 2 * model_width
+    )
+    grad_cross_pair = contract_rows(enc_own, low_pair_two)
+    grad_encoder = times_transposed(
+        low_pair_two, packed_cross[:, model_width : 3 * model_width]
     ).reshape(row_count, enc_block, model_width)
     low_query_two = grad_query_two.reshape(row_count * block_len, model_width)
     grad_cross_query = contract_rows(norm_two, low_query_two)
     grad_norm_two = times_transposed(low_query_two, cross_back[1])
+    summed_cross = scatter_rows(
+        jnp.concatenate([grad_cross_query, grad_cross_pair, grad_cross_out], axis=1).astype(
+            jnp.bfloat16
+        )
+    )
     grad_residual_two, grad_gain_two = rms_backward(
         hidden_one, factor_two, cross_back[0], grad_norm_two
     )
@@ -293,91 +327,55 @@
     grad_table = jnp.einsum(
         "qbk,rhqk->bh", onehot.astype(jnp.float32), grad_scores_one, precision=highest
     )
-    grad_key_one, grad_value_one = (
-        lax.psum_scatter(
-            grad_key_part_one.reshape(row_count, full_len, model_width).astype(jnp.bfloat16),
-            "seq",
-            scatter_dimension=1,
-            tiled=True,
-        ).astype(jnp.float32),
-        lax.psum_scatter(
-            grad_value_part_one.reshape(row_count, full_len, model_width).astype(jnp.bfloat16),
-            "seq",
-            scatter_dimension=1,
-            tiled=True,
-        ).astype(jnp.float32),
-    )
-    low_key_one = grad_key_one.astype(jnp.bfloat16).reshape(row_count * block_len, model_width)
-    low_value_one = grad_value_one.astype(jnp.bfloat16).reshape(row_count * block_len, model_width)
+    pair_one = jnp.concatenate(
+        [
+            grad_key_part_one.reshape(row_count, full_len, model_width),
+            grad_value_part_one.reshape(row_count, full_len, model_width),
+        ],
+        axis=2,
+    ).astype(jnp.bfloat16)
+    low_pair_one = scatter_to_owner(pair_one, row_count, block_len).reshape(
+        row_count * block_len, 2 * model_width
+    )
     low_query_one = grad_query_one.reshape(row_count * block_len, model_width)
-    grad_self_query = contract_rows(norm_one, low_query_one)
-    grad_self_key = contract_rows(norm_one, low_key_one)
-    grad_self_value = contract_rows(norm_one, low_value_one)
-    grad_norm_one = (
-        times_transposed(low_query_one, self_back[1])
-        + times_transposed(low_key_one, self_back[2])
-        + times_transposed(low_value_one, self_back[3])
-    )
+    low_qkv_one = jnp.concatenate([low_query_one, low_pair_one], axis=1)
+    grad_self_qkv = contract_rows(norm_one, low_qkv_one)
+    grad_norm_one = times_transposed(low_qkv_one, packed_self[:, : 3 * model_width])
     grad_residual_one, grad_gain_one = rms_backward(
         inputs_flat, factor_one, self_back[0], grad_norm_one
     )
     grad_tokens = (grad_one + grad_residual_one).reshape(row_count, block_len, model_width)
-    summed = (
-        lax.psum_scatter(grad_gain_one, ("fsdp", "seq"), scatter_dimension=0, tiled=True),
-        lax.psum_scatter(
-            grad_self_query.reshape(-1), ("fsdp", "seq"), scatter_dimension=0, tiled=True
-        ),
-        lax.psum_scatter(
-            grad_self_key.reshape(-1), ("fsdp", "seq"), scatter_dimension=0, tiled=True
-        ),
-        lax.psum_scatter(
-            grad_self_value.reshape(-1), ("fsdp", "seq"), scatter_dimension=0, tiled=True
-        ),
-        lax.psum_scatter(
-            grad_self_out.reshape(-1), ("fsdp", "seq"), scatter_dimension=0, tiled=True
-        ),
-        lax.psum_scatter(grad_gain_two, ("fsdp", "seq"), scatter_dimension=0, tiled=True),
-        lax.psum_scatter(
-            grad_cross_query.reshape(-1), ("fsdp", "seq"), scatter_dimension=0, tiled=True
-        ),
-        lax.psum_scatter(
-            grad_cross_key.reshape(-1), ("fsdp", "seq"), scatter_dimension=0, tiled=True
-        ),
-        lax.psum_scatter(
-            grad_cross_value.reshape(-1), ("fsdp", "seq"), scatter_dimension=0, tiled=True
-        ),
-        lax.psum_scatter(
-            grad_cross_out.reshape(-1), ("fsdp", "seq"), scatter_dimension=0, tiled=True
-        ),
-        lax.psum_scatter(grad_gain_three, ("fsdp", "seq"), scatter_dimension=0, tiled=True),
-        lax.psum_scatter(
-            grad_gate_weight.reshape(-1), ("fsdp", "seq"), scatter_dimension=0, tiled=True
-        ),
-        lax.psum_scatter(
-            grad_up_weight.reshape(-1), ("fsdp", "seq"), scatter_dimension=0, tiled=True
-        ),
-        lax.psum_scatter(grad_down.reshape(-1), ("fsdp", "seq"), scatter_dimension=0, tiled=True),
-    )
-    table_grad = lax.psum(grad_table, ("fsdp", "seq"))
+    summed_self = scatter_rows(
+        jnp.concatenate([grad_self_qkv, grad_self_out], axis=1).astype(jnp.bfloat16)
+    )
+    table_items = grad_table.size
+    small_parts = jnp.concatenate(
+        [grad_table.reshape(-1), grad_gain_one, grad_gain_two, grad_gain_three]
+    )
+    small_sum = sum_everywhere(small_parts.reshape(-1, 128)).reshape(-1)
+    table_grad = small_sum[:table_items].reshape(grad_table.shape)
+    own_index = lax.axis_index("fsdp") * seq_count + seq_index
+
+    def flat_columns(summed, start, width):
+        return summed[:, start : start + width].reshape(-1).astype(jnp.float32)
+
+    def gain_grad(index):
+        start = table_items + index * model_width + own_index * own_rows
+        return lax.dynamic_slice_in_dim(small_sum, start, own_rows, 0)
+
     return (
         output,
         grad_tokens,
         grad_encoder,
-        summed[0],
-        summed[1],
-        summed[2],
-        summed[3],
-        summed[4],
+        gain_grad(0),
+        *[flat_columns(summed_self, index * model_width, model_width) for index in range(4)],
         table_grad,
-        summed[5],
-        summed[6],
-        summed[7],
-        summed[8],
-        summed[9],
-        summed[10],
-        summed[11],
-        summed[12],
-        summed[13],
+        gain_grad(1),
+        *[flat_columns(summed_cross, index * model_width, model_width) for index in range(4)],
+        gain_grad(2),
+        flat_columns(summed_in, 0, hidden_width),
+        flat_columns(summed_in, hidden_width, hidden_width),
+        summed_down.reshape(-1).astype(jnp.float32),
     )
 
 

time: 1400 us -> 735 us (0.53)
  local copies, waits for them, and re-layouts: 570 us -> 42.4 us
  blocking collectives: 105 us -> 0 us
  waiting for transfers between devices: 595 us -> 559 us
  matrix products: 91 us -> 74.8 us
    unnamed x21 -> x8, waiting for transfers between devices: 518 us -> 0.13 us
    gather x2 -> x0, local copies, waits for them, and re-layouts: 408 us -> none  [per_device(): bucket_at = jnp.take(buckets, jnp.clip(distance, 0, full_len - 1))]
    reduce_scatter x0 -> x4, waiting for transfers between devices: none -> 319 us  [scatter_rows(): lax.psum_scatter(partial, ('fsdp', 'seq'), scatter_dimension=0, tiled=True)]
    all_gather x11 -> x4, waiting for transfers between devices: 77 us -> 207 us  [the longest x3 190 us: gather_rows(): return lax.all_gather(packed, ('fsdp', 'seq'), axis=0, tiled=True)]
    unnamed x2 -> x0, blocking collectives: 83.3 us -> none
    reshape x20 -> x13, local copies, waits for them, and re-layouts: 73.2 us -> 6.03 us  [the longest x10 3.61 us: rows_of(): return flat.reshape(own_rows, -1)]
    unnamed x207 -> x202, local copies, waits for them, and re-layouts: 66.8 us -> 12.6 us
    ppermute x0 -> x11, waiting for transfers between devices: none -> 32.4 us  [the longest x6 26.9 us: scatter_to_owner(): total = total + lax.ppermute(piece, 'seq', pairs).astype(jnp.float32)]
  transfers between devices with their start and end apart: 16 -> 19, of which waited for: 3 -> 17; matrix products, arithmetic and copies ran while one was open for 44% -> 15% of each run, Pallas kernels for 0% -> 0%
where the time goes in v1:
time: 735 us; the launch traced here: 730 us
  waiting for transfers between devices  559 us (76%)
  matrix products  74.8 us (10%)
  local copies, waits for them, and re-layouts  42.4 us (6%)
  other arithmetic  24.3 us (3%)
  between operations  16.1 us (2%)
  starting transfers between devices  13.7 us (2%)
    reduce_scatter x4, waiting for transfers between devices, scatter_rows(): lax.psum_scatter(partial, ('fsdp', 'seq'), scatter_dimension=0, tiled=True)  319 us
    all_gather x3, waiting for transfers between devices, gather_rows(): return lax.all_gather(packed, ('fsdp', 'seq'), axis=0, tiled=True)  190 us
    ppermute x6, waiting for transfers between devices, scatter_to_owner(): total = total + lax.ppermute(piece, 'seq', pairs).astype(jnp.float32)  26.9 us
    dot_general x7, matrix products, times_transposed(): lax.dot_general(first_op, second_op, (((1,), (1,)), ((), ())), preferred_...  22.6 us
    all_gather x1, waiting for transfers between devices, per_device(): lax.all_gather(qkv_one[:, model_width:].reshape(row_count, block_len, 2 *...  16.5 us
  transfers between devices with their start and end apart: 19, of which 17 were waited for; matrix products, arithmetic and copies ran while one was open for 15% of the time, Pallas kernels for 0%

profile of v1, /device:TPU:0, one launch (start us, length us, event | category | flops | bytes accessed | tf_op | source)
XLA Modules:
  0.0 729.8 jit_solution(9494032237790957650)
XLA Ops:
  12.2 1.6 reshape.634
  13.9 1.0 fusion.52
  15.5 63.9 %all-gather.6.cloned.1.call-done = bf16[768,3200]{1,0:T(8,128)(2,1)} async-done(((bf16[24,3200]{1,0:T(8,128)(2,1)}), bf16[768,3200]{1,0:T(8,128)(2,1)}) %all-gather.6.cloned.1.call-update) | async-done | bytes 4915216 | tf_op jit(solution)/shard_map/all_gather | solution.py:45
  79.4 2.1 convert_reduce_fusion
  81.5 2.9 convolution_convert_fusion.2
  87.6 3.9 fusion.1
  91.5 5.2 copy.111
  97.0 43.8 %all-gather.10.cloned.1.call-done = bf16[2048,768]{1,0:T(8,128)(2,1)} async-done(((bf16[64,768]{1,0:T(8,128)(2,1)}), bf16[2048,768]{1,0:T(8,128)(2,1)}) %all-gather.10.cloned.1.call-update) | async-done | bytes 3145744 | tf_op jit(solution)/shard_map/all_gather | solution.py:45
  140.7 4.0 fusion.75
  144.9 16.5 %all-gather.12.cloned.1.call-done = bf16[512,1536]{1,0:T(8,128)(2,1)} async-done(((bf16[128,1536]{1,0:T(8,128)(2,1)}), bf16[512,1536]{1,0:T(8,128)(2,1)}) %all-gather.12.cloned.1.call-update) | async-done | bytes 1572880 | tf_op jit(solution)/shard_map/all_gather | solution.py:222
  161.4 1.5 fusion.95
  163.5 2.9 fusion.97
  168.2 1.8 multiply_reduce_fusion.7
  170.6 82.5 %all-gather.8.cloned.1.call-done = bf16[768,7168]{1,0:T(8,128)(2,1)} async-done(((bf16[24,7168]{1,0:T(8,128)(2,1)}), bf16[768,7168]{1,0:T(8,128)(2,1)}) %all-gather.8.cloned.1.call-update) | async-done | bytes 11010064 | tf_op jit(solution)/shard_map/all_gather | solution.py:45
  253.1 1.6 convolution_convert_fusion.19
  254.9 2.2 convolution_convert_fusion.8
  258.9 2.0 copy-done.23
  264.5 1.4 fusion.36
  266.0 2.8 multiply_reduce_fusion.2
  268.8 2.9 convolution_convert_fusion.4
  272.0 1.9 convolution_convert_fusion.17
  274.1 3.6 multiply_reduce_fusion.1
  279.1 0.9 convolution_convert_fusion.10
  280.1 1.1 fusion.64
  281.5 1.5 collective-permute-start.4
  282.9 1.2 collective-permute-start.5
  285.5 1.6 convolution_convert_fusion.5
  287.0 2.4 copy.119
  289.4 1.4 convolution_convert_fusion.6
  290.8 1.3 collective-permute-done.3
  292.1 1.6 collective-permute-done.4
  293.7 6.6 collective-permute-done.5
  300.3 1.5 fusion.51
  302.6 2.6 pad_maximum_fusion.1
  305.3 2.8 multiply_reduce_fusion.3
  308.1 1.3 subtract_add_fusion
  310.1 2.5 convolution_convert_fusion.15
  312.6 1.7 copy.114
  314.4 2.3 multiply_reduce_fusion
  320.6 1.5 collective-permute-start.1
  323.6 10.7 %collective-permute-done = bf16[1,128,1536]{1,2,0:T(8,128)(2,1)S(1)} collective-permute-done((bf16[1,128,1536]{1,2,0:T(8,128)(2,1)S(1)}, bf16[1,128,1536]{1,2,0:T(8,128)(2,1)S(1)}, u32[]{:S(2)}, u32[]{:S(2)}) %collective-permute-start) | collective-permute-done | bytes 393248 | tf_op jit(solution)/shard_map/ppermute | solution.py:60
  335.1 5.9 collective-permute-done.2
  341.3 1.2 convolution_convert_fusion.1
  342.5 2.8 pad_maximum_fusion
  346.6 4.5 convolution_convert_fusion
  351.1 1.9 copy-done.7
  353.0 3.5 copy.115
  356.5 6.5 fusion.29
  363.7 5.0 fusion.61
  370.0 2.0 collective-permute-start.6
  372.0 1.0 collective-permute-done.6
  374.2 2.3 fusion.28
  376.5 1.1 collective-permute-done.7
  377.6 1.5 collective-permute-start.8
  379.1 3.4 fusion.22
  382.6 1.5 collective-permute-start.9
  384.1 2.2 collective-permute-done.9
  386.3 2.4 collective-permute-start.10
  389.6 1.2 collective-permute-done.10
  392.3 1.7 reshape.664
  393.9 94.4 %reduce-scatter.7.cloned.1.call-done = bf16[24,3072]{1,0:T(8,128)(2,1)} async-done(((bf16[768,3072]{1,0:T(8,128)(2,1)}), bf16[24,3072]{1,0:T(8,128)(2,1)}) %reduce-scatter.7.cloned.1.call-update) | async-done | bytes 147472 | tf_op jit(solution)/shard_map/reduce_scatter | solution.py:49
  491.7 109.0 %reduce-scatter.5.cloned.1.call-done = bf16[24,3072]{1,0:T(8,128)(2,1)} async-done(((bf16[768,3072]{1,0:T(8,128)(2,1)}), bf16[24,3072]{1,0:T(8,128)(2,1)}) %reduce-scatter.5.cloned.1.call-update) | async-done | bytes 147472 | tf_op jit(solution)/shard_map/reduce_scatter | solution.py:49
  604.1 116.0 %reduce-scatter.9.cloned.1.call-done = bf16[24,4096]{1,0:T(8,128)(2,1)} async-done(((bf16[768,4096]{1,0:T(8,128)(2,1)}), bf16[24,4096]{1,0:T(8,128)(2,1)}) %reduce-scatter.9.cloned.1.call-update) | async-done | bytes 196624 | tf_op jit(solution)/shard_map/reduce_scatter | solution.py:49
  720.1 1.0 convert_bitcast_fusion
  (300 shorter events, 43.3 us)
Async XLA Ops:
  7.2 247.7 %copy-start = (bf16[1,512,768]{2,1,0:T(8,128)(2,1)S(1)}, bf16[1,512,768]{2,1,0:T(8,128)(2,1)}, u32[]{:S(2)}) copy-start(bf16[1,512,768]{2,1,0:T(8,128)(2,1)} %param.22) | copy-start | bytes 2359300
  7.2 72.2 %all-gather.6.cloned.1.call-start = ((), (), s32[]{:S(2)}) async-start(), calls=%async_computation.4 | async-start | bytes 5068800 | tf_op jit(solution)/shard_map/all_gather | solution.py:45
  12.2 128.6 %all-gather.10.cloned.1.call-start = ((), (), s32[]{:S(2)}) async-start(), calls=%async_computation.6 | async-start | bytes 3244032 | tf_op jit(solution)/shard_map/all_gather | solution.py:45
  13.9 147.5 %all-gather.12.cloned.1.call-start = ((), (), s32[]{:S(2)}) async-start(), calls=%async_computation.11 | async-start | bytes 1966080 | tf_op jit(solution)/shard_map/all_gather | solution.py:222
  15.5 69.7 %copy-start.84 = (f32[128]{0:T(128)}, f32[128]{0:T(128)S(1)}, u32[]{:S(2)}) copy-start(f32[128]{0:T(128)S(1)} %get-tuple-element.126) | copy-start | bytes 1540
  81.5 171.6 %copy-start.59 = (f32[768]{0:T(1024)}, f32[768]{0:T(1024)S(1)}, u32[]{:S(2)}) copy-start(f32[768]{0:T(1024)S(1)} %get-tuple-element.91) | copy-start | bytes 9220
  81.5 4.0 copy-start.71
  81.5 4.1 copy-start.57
  81.5 4.1 copy-start.58
  85.2 167.9 %all-gather.8.cloned.1.call-start = ((), (), s32[]{:S(2)}) async-start(), calls=%async_computation.5 | async-start | bytes 11354112 | tf_op jit(solution)/shard_map/all_gather | solution.py:45
  86.5 305.7 %reduce-scatter.11.cloned.1.call-start = ((), (), s32[]{:S(2)}) async-start(), calls=%async_computation.10 | async-start | bytes 3244032 | tf_op jit(solution)/shard_map/reduce_scatter | solution.py:49
  86.9 9.8 %copy-start.55 = (s32[128,512]{0,1:T(8,128)}, s32[128,512]{0,1:T(8,128)S(1)}, u32[]{:S(2)}) copy-start(s32[128,512]{0,1:T(8,128)S(1)} %copy.110) | copy-start | bytes 786436
  91.5 5.2 copy-start.78
  91.5 5.3 copy-start.77
  91.5 49.2 %copy-start.39 = (bf16[1,128,768]{2,1,0:T(8,128)(2,1)S(1)}, bf16[1,128,768]{2,1,0:T(8,128)(2,1)}, u32[]{:S(2)}) copy-start(bf16[1,128,768]{2,1,0:T(8,128)(2,1)} %param.41) | copy-start | bytes 589828
  97.0 164.8 %copy-start.24 = (pred[128,512]{1,0:T(8,128)(4,1)}, pred[128,512]{1,0:T(8,128)(4,1)S(1)}, u32[]{:S(2)}) copy-start(pred[128,512]{1,0:T(8,128)(4,1)S(1)} %get-tuple-element.131) | copy-start | bytes 196612
  144.9 18.5 %copy-start.34 = (bf16[128,768]{0,1:T(8,128)(2,1)}, bf16[128,768]{0,1:T(8,128)(2,1)S(1)}, u32[]{:S(2)}) copy-start(bf16[128,768]{0,1:T(8,128)(2,1)S(1)} %copy.108) | copy-start | bytes 589828
  163.4 91.5 %copy-start.9 = (bf16[1,512,768]{1,2,0:T(8,128)(2,1)}, bf16[1,512,768]{1,2,0:T(8,128)(2,1)S(1)}, u32[]{:S(2)}) copy-start(bf16[1,512,768]{1,2,0:T(8,128)(2,1)S(1)} %copy.107) | copy-start | bytes 2359300
  168.2 86.5 %copy-start.30 = (bf16[12,64,128]{2,1,0:T(8,128)(2,1)}, bf16[12,64,128]{2,1,0:T(8,128)(2,1)S(1)}, u32[]{:S(2)}) copy-start(bf16[12,64,128]{2,1,0:T(8,128)(2,1)S(1)} %convolution_convert_fusion.20) | copy-start | bytes 589828
  170.0 114.8 %copy-start.16 = (f32[128,768]{1,0:T(8,128)}, f32[128,768]{1,0:T(8,128)S(1)}, u32[]{:S(2)}) copy-start(f32[128,768]{1,0:T(8,128)S(1)} %get-tuple-element.136) | copy-start | bytes 1179652
  170.6 87.3 %copy-start.82 = (f32[128]{0:T(128)}, f32[128]{0:T(128)S(1)}, u32[]{:S(2)}) copy-start(f32[128]{0:T(128)S(1)} %get-tuple-element.128) | copy-start | bytes 1540
  254.9 6.0 copy-start.23
  257.9 8.0 %copy-start.4 = (f32[12,128,512]{2,1,0:T(8,128)}, f32[12,128,512]{2,1,0:T(8,128)S(1)}, u32[]{:S(2)}) copy-start(f32[12,128,512]{2,1,0:T(8,128)S(1)} %get-tuple-element.138) | copy-start | bytes 9437188
  271.8 216.6 %reduce-scatter.7.cloned.1.call-start = ((), (), s32[]{:S(2)}) async-start(), calls=%async_computation.8 | async-start | bytes 4866048 | tf_op jit(solution)/shard_map/reduce_scatter | solution.py:49
  272.0 17.4 %copy-start.15 = (f32[128,768]{1,0:T(8,128)}, f32[128,768]{1,0:T(8,128)S(1)}, u32[]{:S(2)}) copy-start(f32[128,768]{1,0:T(8,128)S(1)} %subtract_add_fusion.1) | copy-start | bytes 1179652
  279.1 5.0 copy-start.19
  280.1 5.4 copy-start.60
  280.1 5.4 copy-start.83
  281.2 10.9 %collective-permute-start.3 = (bf16[1,128,1536]{1,2,0:T(8,128)(2,1)}, bf16[1,128,1536]{1,2,0:T(8,128)(2,1)}, u32[]{:S(2)}, u32[]{:S(2)}) collective-permute-start(bf16[1,128,1536]{1,2,0:T(8,128)(2,1)} %get-tuple-element.104), channel_id=1, source_target_pairs={{0,1},{1,2},{2,3},{3,0},{4,5},{5,6},{6,7},{7,4},{8,9},{9,10},{10,1... | collective-permute-start | bytes 1179656 | tf_op jit(solution)/shard_map/ppermute | solution.py:60
  281.5 12.3 %collective-permute-start.4 = (bf16[1,128,1536]{1,2,0:T(8,128)(2,1)}, bf16[1,128,1536]{1,2,0:T(8,128)(2,1)}, u32[]{:S(2)}, u32[]{:S(2)}) collective-permute-start(bf16[1,128,1536]{1,2,0:T(8,128)(2,1)} %get-tuple-element.105), channel_id=1, source_target_pairs={{0,2},{1,3},{2,0},{3,1},{4,6},{5,7},{6,4},{7,5},{8,10},{9,11},{10,... | collective-permute-start | bytes 1179656 | tf_op jit(solution)/shard_map/ppermute | solution.py:60
  282.9 17.4 %collective-permute-start.5 = (bf16[1,128,1536]{1,2,0:T(8,128)(2,1)}, bf16[1,128,1536]{1,2,0:T(8,128)(2,1)}, u32[]{:S(2)}, u32[]{:S(2)}) collective-permute-start(bf16[1,128,1536]{1,2,0:T(8,128)(2,1)} %get-tuple-element.106), channel_id=1, source_target_pairs={{0,3},{1,0},{2,1},{3,2},{4,7},{5,4},{6,5},{7,6},{8,11},{9,8},{10,9... | collective-permute-start | bytes 1179656 | tf_op jit(solution)/shard_map/ppermute | solution.py:60
  290.8 11.8 %copy-start.17 = (bf16[768,768]{1,0:T(8,128)(2,1)S(1)}, bf16[768,768]{1,0:T(8,128)(2,1)}, u32[]{:S(2)}) copy-start(bf16[768,768]{1,0:T(8,128)(2,1)} %copy.119) | copy-start | bytes 3538948
  305.2 9.2 %copy-start.3 = (f32[12,128,512]{2,1,0:T(8,128)S(1)}, f32[12,128,512]{2,1,0:T(8,128)}, u32[]{:S(2)}) copy-start(f32[12,128,512]{2,1,0:T(8,128)} %copy-done.2) | copy-start | bytes 9437188
  305.2 295.5 %reduce-scatter.5.cloned.1.call-start = ((), (), s32[]{:S(2)}) async-start(), calls=%async_computation.7 | async-start | bytes 4866048 | tf_op jit(solution)/shard_map/reduce_scatter | solution.py:49
  317.6 5.3 copy-start.6
  319.7 14.6 %collective-permute-start = (bf16[1,128,1536]{1,2,0:T(8,128)(2,1)S(1)}, bf16[1,128,1536]{1,2,0:T(8,128)(2,1)S(1)}, u32[]{:S(2)}, u32[]{:S(2)}) collective-permute-start(bf16[1,128,1536]{1,2,0:T(8,128)(2,1)S(1)} %get-tuple-element.107), channel_id=1, source_target_pairs={{0,1},{1,2},{2,3},{3,0},{4,5},{5,6},{6,7},{7,4},{8,9},{9,10},{10,1... | collective-permute-start | bytes 1179656 | tf_op jit(solution)/shard_map/ppermute | solution.py:60
  320.6 14.5 %collective-permute-start.1 = (bf16[1,128,1536]{1,2,0:T(8,128)(2,1)S(1)}, bf16[1,128,1536]{1,2,0:T(8,128)(2,1)S(1)}, u32[]{:S(2)}, u32[]{:S(2)}) collective-permute-start(bf16[1,128,1536]{1,2,0:T(8,128)(2,1)S(1)} %get-tuple-element.108), channel_id=1, source_target_pairs={{0,2},{1,3},{2,0},{3,1},{4,6},{5,7},{6,4},{7,5},{8,10},{9,11},{10,... | collective-permute-start | bytes 1179656 | tf_op jit(solution)/shard_map/ppermute | solution.py:60
  322.1 18.9 %collective-permute-start.2 = (bf16[1,128,1536]{1,2,0:T(8,128)(2,1)S(1)}, bf16[1,128,1536]{1,2,0:T(8,128)(2,1)S(1)}, u32[]{:S(2)}, u32[]{:S(2)}) collective-permute-start(bf16[1,128,1536]{1,2,0:T(8,128)(2,1)S(1)} %get-tuple-element.109), channel_id=1, source_target_pairs={{0,3},{1,0},{2,1},{3,2},{4,7},{5,4},{6,5},{7,6},{8,11},{9,8},{10,9... | collective-permute-start | bytes 1179656 | tf_op jit(solution)/shard_map/ppermute | solution.py:60
  322.9 18.4 %copy-start.21 = (bf16[1,128,768]{2,1,0:T(8,128)(2,1)S(1)}, bf16[1,128,768]{2,1,0:T(8,128)(2,1)}, u32[]{:S(2)}) copy-start(bf16[1,128,768]{2,1,0:T(8,128)(2,1)} %param.21) | copy-start | bytes 589828
  322.9 18.4 %copy-start.73 = (f32[768]{0:T(1024)S(1)}, f32[768]{0:T(1024)}, u32[]{:S(2)}) copy-start(f32[768]{0:T(1024)} %copy-done.72) | copy-start | bytes 9220
  322.9 18.4 %copy-start.85 = (f32[128]{0:T(128)S(1)}, f32[128]{0:T(128)}, u32[]{:S(2)}) copy-start(f32[128]{0:T(128)} %copy-done.84) | copy-start | bytes 1540
  323.6 18.9 %copy-start.47 = (bf16[12,64,128]{2,1,0:T(8,128)(2,1)}, bf16[12,64,128]{2,1,0:T(8,128)(2,1)S(1)}, u32[]{:S(2)}) copy-start(bf16[12,64,128]{2,1,0:T(8,128)(2,1)S(1)} %convolution_convert_fusion.14) | copy-start | bytes 589828
  345.3 374.8 %reduce-scatter.9.cloned.1.call-start = ((), (), s32[]{:S(2)}) async-start(), calls=%async_computation.9 | async-start | bytes 6488064 | tf_op jit(solution)/shard_map/reduce_scatter | solution.py:49
  363.7 5.6 copy-start.63
  363.7 5.6 copy-start.64
  363.7 5.6 copy-start.75
  363.7 10.5 %copy-start.8 = (bf16[2048,768]{1,0:T(8,128)(2,1)S(1)}, bf16[2048,768]{1,0:T(8,128)(2,1)}, u32[]{:S(2)}) copy-start(bf16[2048,768]{1,0:T(8,128)(2,1)} %all-gather.10.cloned.1.call-done) | copy-start | bytes 9437188
  370.0 3.0 collective-permute-start.6
  372.0 5.6 copy-start.65
  372.0 5.6 copy-start.67
  372.0 5.6 copy-start.76
  372.0 7.2 copy-start.42
  373.7 10.3 %copy-start.94 = (f32[128]{0:T(128)S(1)}, f32[128]{0:T(128)}, u32[]{:S(2)}) copy-start(f32[128]{0:T(128)} %get-tuple-element.98) | copy-start | bytes 1540
  373.7 14.9 %copy-start.14 = (f32[128,768]{1,0:T(8,128)S(1)}, f32[128,768]{1,0:T(8,128)}, u32[]{:S(2)}) copy-start(f32[128,768]{1,0:T(8,128)} %copy-done.12) | copy-start | bytes 1179652
  373.8 14.9 %copy-start.22 = (bf16[1,128,768]{2,1,0:T(8,128)(2,1)S(1)}, bf16[1,128,768]{2,1,0:T(8,128)(2,1)}, u32[]{:S(2)}) copy-start(bf16[1,128,768]{2,1,0:T(8,128)(2,1)} %param.21) | copy-start | bytes 589828
  373.8 14.9 %copy-start.54 = (f32[128,768]{1,0:T(8,128)S(1)}, f32[128,768]{1,0:T(8,128)}, u32[]{:S(2)}) copy-start(f32[128,768]{1,0:T(8,128)} %get-tuple-element.147) | copy-start | bytes 1179652
  373.8 14.9 %copy-start.74 = (f32[768]{0:T(1024)S(1)}, f32[768]{0:T(1024)}, u32[]{:S(2)}) copy-start(f32[768]{0:T(1024)} %copy-done.72) | copy-start | bytes 9220
  373.8 14.9 %copy-start.86 = (f32[128]{0:T(128)S(1)}, f32[128]{0:T(128)}, u32[]{:S(2)}) copy-start(f32[128]{0:T(128)} %copy-done.84) | copy-start | bytes 1540
  373.8 14.9 %copy-start.87 = (f32[128]{0:T(128)S(1)}, f32[128]{0:T(128)}, u32[]{:S(2)}) copy-start(f32[128]{0:T(128)} %get-tuple-element.125) | copy-start | bytes 1540
  373.8 3.8 collective-permute-start.7
  377.6 5.0 collective-permute-start.8
  379.1 343.4 %copy-start.1 = (bf16[1,512,768]{2,1,0:T(8,128)(2,1)S(1)}, bf16[1,512,768]{2,1,0:T(8,128)(2,1)}, u32[]{:S(2)}) copy-start(bf16[1,512,768]{2,1,0:T(8,128)(2,1)} %param.22) | copy-start | bytes 2359300
  382.6 3.7 collective-permute-start.9
  386.3 4.6 collective-permute-start.10
  (50 other events, 111.7 us)
Sparse Core Ops, SparseCore 0:
  12.3 67.0 all-gather.5
  82.8 57.8 all-gather.9
  142.9 18.4 all-gather.11
  164.2 88.8 all-gather.7
  271.9 105.0 reduce-scatter.10
  382.3 105.9 reduce-scatter.6
  494.7 105.9 reduce-scatter.4
  606.4 113.7 reduce-scatter.8

commit v2 on v1

--- a/solution.py
+++ b/solution.py
@@ -59,6 +59,20 @@
         pairs = [(source, (source + step) % count) for source in range(count)]
         total = total + lax.ppermute(piece, "seq", pairs).astype(jnp.float32)
     return total.astype(jnp.bfloat16)
+
+
+def gather_positions(own, full_len):
+    count = lax.axis_size("seq")
+    index = lax.axis_index("seq")
+    block = own.shape[1]
+    full = jnp.zeros((own.shape[0], full_len, own.shape[2]), own.dtype)
+    full = lax.dynamic_update_slice_in_dim(full, own, index * block, 1)
+    for step in range(1, count):
+        pairs = [(source, (source + step) % count) for source in range(count)]
+        origin = lax.rem(index + count - step, count)
+        arrived = lax.ppermute(own, "seq", pairs)
+        full = lax.dynamic_update_slice_in_dim(full, arrived, origin * block, 1)
+    return full
 
 
 def sum_everywhere(values):
@@ -194,20 +208,23 @@
                     cross_output,
                     ffn_gate,
                     ffn_up,
+                    ffn_down,
                 )
             ],
             axis=1,
         )
     )
     packed_cross = packed_rest[:, : 4 * model_width]
-    packed_in = packed_rest[:, 4 * model_width :]
-    packed_down = gather_rows(ffn_down.reshape(-1, model_width))
+    hidden_width = ffn_down.size // own_rows
+    packed_in = packed_rest[:, 4 * model_width : 4 * model_width + 2 * hidden_width]
+    packed_down = packed_rest[:, 4 * model_width + 2 * hidden_width :].reshape(
+        hidden_width, model_width
+    )
     all_gains = packed_self[:, 4 * model_width :]
 
     def columns(packed, index):
         return packed[:, index * model_width : (index + 1) * model_width]
 
-    hidden_width = packed_down.shape[0]
     self_full = [all_gains[:, 0]] + [columns(packed_self, index) for index in range(4)]
     cross_full = [all_gains[:, 1]] + [columns(packed_cross, index) for index in range(4)]
     ffn_full = [
@@ -219,11 +236,8 @@
     norm_one, factor_one = rms_forward(inputs_flat, self_full[0])
     qkv_one = matmul(norm_one, packed_self[:, : 3 * model_width]).astype(jnp.bfloat16)
     query_one = qkv_one[:, :model_width]
-    pair_all = lax.all_gather(
-        qkv_one[:, model_width:].reshape(row_count, block_len, 2 * model_width),
-        "seq",
-        axis=1,
-        tiled=True,
+    pair_all = gather_positions(
+        qkv_one[:, model_width:].reshape(row_count, block_len, 2 * model_width), full_len
     )
     key_all = pair_all[:, :, :model_width]
     value_all = pair_all[:, :, model_width:]
@@ -267,8 +281,15 @@
     low_gate = grad_gate.astype(jnp.bfloat16)
     low_up = grad_up.astype(jnp.bfloat16)
     low_in = jnp.concatenate([low_gate, low_up], axis=1)
-    summed_in = scatter_rows(contract_rows(norm_three, low_in).astype(jnp.bfloat16))
-    summed_down = scatter_rows(grad_down.astype(jnp.bfloat16))
+    summed_ffn = scatter_rows(
+        jnp.concatenate(
+            [
+                contract_rows(norm_three, low_in).astype(jnp.bfloat16),
+                grad_down.astype(jnp.bfloat16).reshape(model_width, hidden_width),
+            ],
+            axis=1,
+        )
+    )
     grad_norm_three = times_transposed(low_in, packed_in)
     grad_residual_three, grad_gain_three = rms_backward(
         hidden_two, factor_three, ffn_back[0], grad_norm_three
@@ -303,11 +324,6 @@
     low_query_two = grad_query_two.reshape(row_count * block_len, model_width)
     grad_cross_query = contract_rows(norm_two, low_query_two)
     grad_norm_two = times_transposed(low_query_two, cross_back[1])
-    summed_cross = scatter_rows(
-        jnp.concatenate([grad_cross_query, grad_cross_pair, grad_cross_out], axis=1).astype(
-            jnp.bfloat16
-        )
-    )
     grad_residual_two, grad_gain_two = rms_backward(
         hidden_one, factor_two, cross_back[0], grad_norm_two
     )
@@ -345,8 +361,11 @@
         inputs_flat, factor_one, self_back[0], grad_norm_one
     )
     grad_tokens = (grad_one + grad_residual_one).reshape(row_count, block_len, model_width)
-    summed_self = scatter_rows(
-        jnp.concatenate([grad_self_qkv, grad_self_out], axis=1).astype(jnp.bfloat16)
+    summed_attention = scatter_rows(
+        jnp.concatenate(
+            [grad_self_qkv, grad_self_out, grad_cross_query, grad_cross_pair, grad_cross_out],
+            axis=1,
+        ).astype(jnp.bfloat16)
     )
     table_items = grad_table.size
     small_parts = jnp.concatenate(
@@ -368,14 +387,12 @@
         grad_tokens,
         grad_encoder,
         gain_grad(0),
-        *[flat_columns(summed_self, index * model_width, model_width) for index in range(4)],
+        *[flat_columns(summed_attention, index * model_width, model_width) for index in range(4)],
         table_grad,
         gain_grad(1),
-        *[flat_columns(summed_cross, index * model_width, model_width) for index in range(4)],
+        *[flat_columns(summed_attention, index * model_width, model_width) for index in range(4, 8)],
         gain_grad(2),
-        flat_columns(summed_in, 0, hidden_width),
-        flat_columns(summed_in, hidden_width, hidden_width),
-        summed_down.reshape(-1).astype(jnp.float32),
+        *[flat_columns(summed_ffn, index * hidden_width, hidden_width) for index in range(3)],
     )
 
 

time: 735 us -> 534 us (0.73)
  waiting for transfers between devices: 559 us -> 340 us
  local copies, waits for them, and re-layouts: 42.4 us -> 62.4 us
  other arithmetic: 24.3 us -> 16.3 us
    reduce_scatter x4 -> x2, waiting for transfers between devices: 319 us -> 158 us  [scatter_rows(): lax.psum_scatter(partial, ('fsdp', 'seq'), scatter_dimension=0, tiled=True)]
    all_gather x3 -> x2, waiting for transfers between devices: 190 us -> 119 us  [gather_rows(): return lax.all_gather(packed, ('fsdp', 'seq'), axis=0, tiled=True)]
    ppermute x0 -> x3, waiting for transfers between devices: none -> 19.3 us  [gather_positions(): arrived = lax.ppermute(own, 'seq', pairs)]
    all_gather x1 -> x0, waiting for transfers between devices: 16.5 us -> none  [per_device(): lax.all_gather(qkv_one[:, model_width:].reshape(row_count, block_len, 2 *...]
    reshape x1 -> x4, local copies, waits for them, and re-layouts: 1.64 us -> 13.6 us  [the longest x1 6.73 us: per_device(): packed_rest[:, 4 * model_width + 2 * hidden_width:]]
    ppermute x6, waiting for transfers between devices: 26.9 us -> 36 us  [scatter_to_owner(): total = total + lax.ppermute(piece, 'seq', pairs).astype(jnp.float32)]
  transfers between devices with their start and end apart: 19 -> 18, of which waited for: 17 -> 16; matrix products, arithmetic and copies ran while one was open for 15% -> 19% of each run, Pallas kernels for 0% -> 0%
where the time goes in v2:
time: 534 us; the launch traced here: 525 us
  waiting for transfers between devices  340 us (64%)
  matrix products  80 us (15%)
  local copies, waits for them, and re-layouts  62.4 us (12%)
  other arithmetic  16.3 us (3%)
  between operations  15.6 us (3%)
  starting transfers between devices  11.5 us (2%)
    reduce_scatter x2, waiting for transfers between devices, scatter_rows(): lax.psum_scatter(partial, ('fsdp', 'seq'), scatter_dimension=0, tiled=True)  158 us
    all_gather x2, waiting for transfers between devices, gather_rows(): return lax.all_gather(packed, ('fsdp', 'seq'), axis=0, tiled=True)  119 us
    ppermute x6, waiting for transfers between devices, scatter_to_owner(): total = total + lax.ppermute(piece, 'seq', pairs).astype(jnp.float32)  36 us
    dot_general x7, matrix products, times_transposed(): lax.dot_general(first_op, second_op, (((1,), (1,)), ((), ())), preferred_...  20.8 us
    ppermute x3, waiting for transfers between devices, gather_positions(): arrived = lax.ppermute(own, 'seq', pairs)  19.3 us
    dot_general x9, matrix products, matmul(): return jnp.dot(first_op, second_op, preferred_element_type=jnp.float32)  18 us
    dot_general x7, matrix products, contract_rows(): lax.dot_general(first_op, second_op, (((0,), (0,)), ((), ())), preferred_...  15.8 us
  transfers between devices with their start and end apart: 18, of which 16 were waited for; matrix products, arithmetic and copies ran while one was open for 19% of the time, Pallas kernels for 0%

profile of v2, /device:TPU:0, one launch (start us, length us, event | category | flops | bytes accessed | tf_op | source)
XLA Modules:
  0.0 525.5 jit_solution(12722561054861423607)
XLA Ops:
  15.5 0.9 reshape.633
  16.5 0.9 reshape.634
  17.4 0.9 reshape.635
  19.8 4.0 fusion.1
  23.8 5.1 copy.123
  29.6 49.8 %all-gather.3.cloned.1.call-done = bf16[768,3200]{1,0:T(8,128)(2,1)} async-done(((bf16[24,3200]{1,0:T(8,128)(2,1)}), bf16[768,3200]{1,0:T(8,128)(2,1)}) %all-gather.3.cloned.1.call-update) | async-done | bytes 4915216 | tf_op jit(solution)/shard_map/all_gather | solution.py:45
  79.4 2.2 convert_reduce_fusion
  81.6 2.7 convolution_convert_fusion.2
  84.3 1.4 collective-permute-start.2
  87.1 11.3 %collective-permute-done.2 = bf16[1,128,1536]{2,1,0:T(8,128)(2,1)} collective-permute-done((bf16[1,128,1536]{2,1,0:T(8,128)(2,1)S(1)}, bf16[1,128,1536]{2,1,0:T(8,128)(2,1)}, u32[]{:S(2)}, u32[]{:S(2)}) %collective-permute-start.2) | collective-permute-done | bytes 393248 | tf_op jit(solution)/shard_map/ppermute | solution.py:73
  98.4 1.2 copy.120
  99.6 8.0 %collective-permute-done.1 = bf16[1,128,1536]{2,1,0:T(8,128)(2,1)} collective-permute-done((bf16[1,128,1536]{2,1,0:T(8,128)(2,1)S(1)}, bf16[1,128,1536]{2,1,0:T(8,128)(2,1)}, u32[]{:S(2)}, u32[]{:S(2)}) %collective-permute-start.1) | collective-permute-done | bytes 393248 | tf_op jit(solution)/shard_map/ppermute | solution.py:73
  107.6 1.9 copy.119
  109.5 1.2 copy.118
  110.9 1.2 constant_dynamic-update-slice_fusion.13
  115.8 1.8 multiply_reduce_fusion.7
  118.1 68.8 %all-gather.5.cloned.1.call-done = bf16[768,9216]{1,0:T(8,128)(2,1)} async-done(((bf16[24,9216]{1,0:T(8,128)(2,1)}), bf16[768,9216]{1,0:T(8,128)(2,1)}) %all-gather.5.cloned.1.call-update) | async-done | bytes 14155792 | tf_op jit(solution)/shard_map/all_gather | solution.py:45
  186.9 4.0 slice.149
  191.0 6.7 %reshape.641 = bf16[2048,768]{1,0:T(8,128)(2,1)} reshape(bf16[768,2048]{1,0:T(8,128)(2,1)} %slice.149) | data formatting | bytes 6291456 | tf_op jit(solution)/shard_map/reshape | solution.py:220
  197.7 1.6 convolution_convert_fusion.19
  199.5 2.2 convolution_convert_fusion.8
  203.4 3.3 convolution_convert_fusion.9
  207.7 1.2 copy-done.19
  210.0 1.1 convolution_bitcast_fusion
  211.9 2.2 fusion.41
  214.1 2.7 convolution_convert_fusion.4
  216.9 6.6 %reshape.657 = bf16[768,2048]{1,0:T(8,128)(2,1)} reshape(bf16[2048,768]{1,0:T(8,128)(2,1)} %convolution_convert_fusion.4) | data formatting | bytes 6291456 | tf_op jit(solution)/shard_map/reshape | solution.py:288
  223.5 3.0 convolution_convert_fusion
  226.5 4.1 pad_maximum_fusion
  231.6 5.7 %multiply_reduce_fusion.2 = (f32[768]{0:T(1024)}, f32[128]{0:T(128)S(1)}, f32[128,768]{1,0:T(8,128)S(1)}) fusion(f32[128,768]{1,0:T(8,128)S(1)} %get-tuple-element.141, f32[128]{0:T(128)S(1)} %get-tuple-element.131, f32[768]{0:T(1024)S(1)} %copy-done.54, bf16[768,9216]{1,0:T(8,128)(2,1)} %all-gather.5.cloned.1.call-done, ...), kind=kOutput, calls=%fused_computation.142 | convolution fusion | flops 807992448 | bytes 8133632 | tf_op jit(solution)/shard_map/dot_general | solution.py:26
  238.2 1.9 convolution_convert_fusion.17
  240.3 3.7 multiply_reduce_fusion.1
  245.9 2.6 multiply_reduce_fusion.3
  249.5 2.5 convolution_convert_fusion.15
  252.0 1.8 copy.127
  253.8 1.3 convolution_convert_fusion.11
  255.1 3.1 convolution_convert_fusion.10
  258.7 1.4 collective-permute-start.7
  260.2 1.2 collective-permute-start.8
  262.1 1.1 multiply_reduce_fusion
  265.5 3.5 collective-permute-done.6
  270.7 7.4 %collective-permute-done.8 = bf16[1,128,1536]{1,2,0:T(8,128)(2,1)S(1)} collective-permute-done((bf16[1,128,1536]{1,2,0:T(8,128)(2,1)S(1)}, bf16[1,128,1536]{1,2,0:T(8,128)(2,1)S(1)}, u32[]{:S(2)}, u32[]{:S(2)}) %collective-permute-start.8) | collective-permute-done | bytes 393248 | tf_op jit(solution)/shard_map/ppermute | solution.py:60
  278.1 10.7 %collective-permute-done.3 = bf16[1,128,1536]{1,2,0:T(8,128)(2,1)S(1)} collective-permute-done((bf16[1,128,1536]{1,2,0:T(8,128)(2,1)S(1)}, bf16[1,128,1536]{1,2,0:T(8,128)(2,1)S(1)}, u32[]{:S(2)}, u32[]{:S(2)}) %collective-permute-start.3) | collective-permute-done | bytes 393248 | tf_op jit(solution)/shard_map/ppermute | solution.py:60
  288.8 3.4 collective-permute-done.4
  292.2 10.4 %collective-permute-done.5 = bf16[1,128,1536]{1,2,0:T(8,128)(2,1)S(1)} collective-permute-done((bf16[1,128,1536]{1,2,0:T(8,128)(2,1)S(1)}, bf16[1,128,1536]{1,2,0:T(8,128)(2,1)S(1)}, u32[]{:S(2)}, u32[]{:S(2)}) %collective-permute-start.5) | collective-permute-done | bytes 393248 | tf_op jit(solution)/shard_map/ppermute | solution.py:60
  303.7 3.0 fusion.4
  306.7 1.6 fusion.26
  308.3 1.7 fusion.25
  310.0 2.3 fusion.11
  312.3 1.6 fusion.24
  313.9 5.2 copy.128
  319.1 6.5 %fusion.34 = f32[32,12]{1,0:T(8,128)S(1)} fusion(f32[12,128,512]{1,0,2:T(8,128)} %copy.128, s32[128,512]{0,1:T(8,128)S(1)} %copy-done.48, s32[32]{0:T(128)S(1)} %copy-done.72, s32[32]{0:T(128)S(1)} %copy-done.70), kind=kOutput, calls=%fused_computation.87 | convolution fusion | flops 308281344 | bytes 3409664 | tf_op jit(solution)/shard_map/qbk,rhqk->bh/dot_general | solution.py:343
  325.8 3.6 fusion.66
  329.4 1.0 collective-permute-start.9
  331.2 1.9 collective-permute-start.10
  333.1 3.2 fusion.33
  336.6 3.3 fusion.27
  340.8 3.2 collective-permute-done.12
  344.1 1.4 collective-permute-start.13
  346.3 3.4 collective-permute-done.13
  351.1 20.0 %reduce-scatter.5.cloned.1.call-done = bf16[24,6144]{1,0:T(8,128)(2,1)} async-done(((bf16[768,6144]{1,0:T(8,128)(2,1)}), bf16[24,6144]{1,0:T(8,128)(2,1)}) %reduce-scatter.5.cloned.1.call-update) | async-done | bytes 294928 | tf_op jit(solution)/shard_map/reduce_scatter | solution.py:49
  371.1 1.0 convert_bitcast_fusion
  374.3 138.2 %reduce-scatter.3.cloned.1.call-done = bf16[24,6144]{1,0:T(8,128)(2,1)} async-done(((bf16[768,6144]{1,0:T(8,128)(2,1)}), bf16[24,6144]{1,0:T(8,128)(2,1)}) %reduce-scatter.3.cloned.1.call-update) | async-done | bytes 294928 | tf_op jit(solution)/shard_map/reduce_scatter | solution.py:49
  512.5 0.9 slice_convert_fusion
  (259 shorter events, 43.2 us)
Async XLA Ops:
  7.2 192.3 %copy-start = (bf16[1,512,768]{2,1,0:T(8,128)(2,1)S(1)}, bf16[1,512,768]{2,1,0:T(8,128)(2,1)}, u32[]{:S(2)}) copy-start(bf16[1,512,768]{2,1,0:T(8,128)(2,1)} %param.22) | copy-start | bytes 2359300
  7.2 12.4 %copy-start.61 = (s32[512]{0:T(512)S(1)}, s32[512]{0:T(512)}, u32[]{:S(2)}) copy-start(s32[512]{0:T(512)} %param.25) | copy-start | bytes 6148
  7.2 12.6 %copy-start.73 = (bf16[32,12]{0,1:T(8,128)(2,1)S(1)}, bf16[32,12]{0,1:T(8,128)(2,1)}, u32[]{:S(2)}) copy-start(bf16[32,12]{0,1:T(8,128)(2,1)} %param.31) | copy-start | bytes 2308
  7.2 72.2 %all-gather.3.cloned.1.call-start = ((), (), s32[]{:S(2)}) async-start(), calls=%async_computation.2 | async-start | bytes 5068800 | tf_op jit(solution)/shard_map/all_gather | solution.py:45
  12.2 174.7 %all-gather.5.cloned.1.call-start = ((), (), s32[]{:S(2)}) async-start(), calls=%async_computation.3 | async-start | bytes 14598144 | tf_op jit(solution)/shard_map/all_gather | solution.py:45
  19.3 351.8 %reduce-scatter.5.cloned.1.call-start = ((), (), s32[]{:S(2)}) async-start(), calls=%async_computation.5 | async-start | bytes 9732096 | tf_op jit(solution)/shard_map/reduce_scatter | solution.py:49
  19.6 9.2 %copy-start.47 = (s32[128,512]{0,1:T(8,128)}, s32[128,512]{0,1:T(8,128)S(1)}, u32[]{:S(2)}) copy-start(s32[128,512]{0,1:T(8,128)S(1)} %copy.122) | copy-start | bytes 786436
  19.8 9.1 %copy-start.69 = (s32[32]{0:T(128)}, s32[32]{0:T(128)S(1)}, u32[]{:S(2)}) copy-start(s32[32]{0:T(128)S(1)} %get-tuple-element.99) | copy-start | bytes 388
  19.8 9.1 %copy-start.71 = (s32[32]{0:T(128)}, s32[32]{0:T(128)S(1)}, u32[]{:S(2)}) copy-start(s32[32]{0:T(128)S(1)} %get-tuple-element.100) | copy-start | bytes 388
  23.8 5.1 copy-start.60
  23.8 5.1 copy-start.35
  29.6 54.7 %copy-start.67 = (f32[128]{0:T(128)}, f32[128]{0:T(128)S(1)}, u32[]{:S(2)}) copy-start(f32[128]{0:T(128)S(1)} %get-tuple-element.127) | copy-start | bytes 1540
  81.6 4.9 copy-start.57
  81.6 116.1 %copy-start.51 = (f32[768]{0:T(1024)}, f32[768]{0:T(1024)S(1)}, u32[]{:S(2)}) copy-start(f32[768]{0:T(1024)S(1)} %get-tuple-element.91) | copy-start | bytes 9220
  81.6 4.7 copy-start.59
  84.3 14.1 %collective-permute-start.2 = (bf16[1,128,1536]{2,1,0:T(8,128)(2,1)S(1)}, bf16[1,128,1536]{2,1,0:T(8,128)(2,1)}, u32[]{:S(2)}, u32[]{:S(2)}) collective-permute-start(bf16[1,128,1536]{2,1,0:T(8,128)(2,1)S(1)} %slice_bitcast_fusion), channel_id=1, source_target_pairs={{0,3},{1,0},{2,1},{3,2},{4,7},{5,4},{6,5},{7,6},{8,11},{9,8},{10,9... | collective-permute-start | bytes 1179656 | tf_op jit(solution)/shard_map/ppermute | solution.py:73
  85.7 21.9 %collective-permute-start.1 = (bf16[1,128,1536]{2,1,0:T(8,128)(2,1)S(1)}, bf16[1,128,1536]{2,1,0:T(8,128)(2,1)}, u32[]{:S(2)}, u32[]{:S(2)}) collective-permute-start(bf16[1,128,1536]{2,1,0:T(8,128)(2,1)S(1)} %slice_bitcast_fusion), channel_id=1, source_target_pairs={{0,2},{1,3},{2,0},{3,1},{4,6},{5,7},{6,4},{7,5},{8,10},{9,11},{10,... | collective-permute-start | bytes 1179656 | tf_op jit(solution)/shard_map/ppermute | solution.py:73
  86.3 23.2 %collective-permute-start = (bf16[1,128,1536]{2,1,0:T(8,128)(2,1)S(1)}, bf16[1,128,1536]{2,1,0:T(8,128)(2,1)}, u32[]{:S(2)}, u32[]{:S(2)}) collective-permute-start(bf16[1,128,1536]{2,1,0:T(8,128)(2,1)S(1)} %slice_bitcast_fusion), channel_id=1, source_target_pairs={{0,1},{1,2},{2,3},{3,0},{4,5},{5,6},{6,7},{7,4},{8,9},{9,10},{10,1... | collective-permute-start | bytes 1179656 | tf_op jit(solution)/shard_map/ppermute | solution.py:73
  86.5 120.3 %copy-start.22 = (pred[128,512]{1,0:T(8,128)(4,1)}, pred[128,512]{1,0:T(8,128)(4,1)S(1)}, u32[]{:S(2)}) copy-start(pred[128,512]{1,0:T(8,128)(4,1)S(1)} %get-tuple-element.132) | copy-start | bytes 196612
  86.9 25.4 %copy-start.30 = (bf16[128,768]{0,1:T(8,128)(2,1)}, bf16[128,768]{0,1:T(8,128)(2,1)S(1)}, u32[]{:S(2)}) copy-start(bf16[128,768]{0,1:T(8,128)(2,1)S(1)} %copy.121) | copy-start | bytes 589828
  115.8 75.2 %copy-start.27 = (bf16[12,64,128]{2,1,0:T(8,128)(2,1)}, bf16[12,64,128]{2,1,0:T(8,128)(2,1)S(1)}, u32[]{:S(2)}) copy-start(bf16[12,64,128]{2,1,0:T(8,128)(2,1)S(1)} %convolution_convert_fusion.20) | copy-start | bytes 589828
  117.6 90.1 %copy-start.16 = (f32[128,768]{1,0:T(8,128)}, f32[128,768]{1,0:T(8,128)S(1)}, u32[]{:S(2)}) copy-start(f32[128,768]{1,0:T(8,128)S(1)} %get-tuple-element.137) | copy-start | bytes 1179652
  118.1 79.5 %copy-start.62 = (f32[128]{0:T(128)}, f32[128]{0:T(128)S(1)}, u32[]{:S(2)}) copy-start(f32[128]{0:T(128)S(1)} %get-tuple-element.129) | copy-start | bytes 1540
  201.7 7.2 %copy-start.19 = (bf16[768,9216]{1,0:T(8,128)(2,1)S(1)}, bf16[768,9216]{1,0:T(8,128)(2,1)}, u32[]{:S(2)}) copy-start(bf16[768,9216]{1,0:T(8,128)(2,1)} %all-gather.5.cloned.1.call-done) | copy-start | bytes 42467332
  202.4 4.3 copy-start.3
  214.1 9.3 %copy-start.25 = (bf16[128,2048]{1,0:T(8,128)(2,1)}, bf16[128,2048]{1,0:T(8,128)(2,1)S(1)}, u32[]{:S(2)}) copy-start(bf16[128,2048]{1,0:T(8,128)(2,1)S(1)} %get-tuple-element.103) | copy-start | bytes 1572868
  230.6 281.9 %reduce-scatter.3.cloned.1.call-start = ((), (), s32[]{:S(2)}) async-start(), calls=%async_computation.4 | async-start | bytes 9732096 | tf_op jit(solution)/shard_map/reduce_scatter | solution.py:49
  240.3 3.7 copy-start.32
  240.3 3.7 copy-start.4
  240.3 3.7 copy-start.24
  255.1 6.3 %copy-start.2 = (f32[12,128,512]{2,1,0:T(8,128)S(1)}, f32[12,128,512]{2,1,0:T(8,128)}, u32[]{:S(2)}) copy-start(f32[12,128,512]{2,1,0:T(8,128)} %copy-done.1) | copy-start | bytes 9437188
  255.1 6.3 %copy-start.33 = (bf16[128,768]{0,1:T(8,128)(2,1)S(1)}, bf16[128,768]{0,1:T(8,128)(2,1)}, u32[]{:S(2)}) copy-start(bf16[128,768]{0,1:T(8,128)(2,1)} %copy.127) | copy-start | bytes 589828
  258.4 10.6 %collective-permute-start.6 = (bf16[1,128,1536]{1,2,0:T(8,128)(2,1)S(1)}, bf16[1,128,1536]{1,2,0:T(8,128)(2,1)S(1)}, u32[]{:S(2)}, u32[]{:S(2)}) collective-permute-start(bf16[1,128,1536]{1,2,0:T(8,128)(2,1)S(1)} %get-tuple-element.104), channel_id=1, source_target_pairs={{0,1},{1,2},{2,3},{3,0},{4,5},{5,6},{6,7},{7,4},{8,9},{9,10},{10,1... | collective-permute-start | bytes 1179656 | tf_op jit(solution)/shard_map/ppermute | solution.py:60
  258.7 12.0 %collective-permute-start.7 = (bf16[1,128,1536]{1,2,0:T(8,128)(2,1)S(1)}, bf16[1,128,1536]{1,2,0:T(8,128)(2,1)S(1)}, u32[]{:S(2)}, u32[]{:S(2)}) collective-permute-start(bf16[1,128,1536]{1,2,0:T(8,128)(2,1)S(1)} %get-tuple-element.105), channel_id=1, source_target_pairs={{0,2},{1,3},{2,0},{3,1},{4,6},{5,7},{6,4},{7,5},{8,10},{9,11},{10,... | collective-permute-start | bytes 1179656 | tf_op jit(solution)/shard_map/ppermute | solution.py:60
  260.2 17.9 %collective-permute-start.8 = (bf16[1,128,1536]{1,2,0:T(8,128)(2,1)S(1)}, bf16[1,128,1536]{1,2,0:T(8,128)(2,1)S(1)}, u32[]{:S(2)}, u32[]{:S(2)}) collective-permute-start(bf16[1,128,1536]{1,2,0:T(8,128)(2,1)S(1)} %get-tuple-element.106), channel_id=1, source_target_pairs={{0,3},{1,0},{2,1},{3,2},{4,7},{5,4},{6,5},{7,6},{8,11},{9,8},{10,9... | collective-permute-start | bytes 1179656 | tf_op jit(solution)/shard_map/ppermute | solution.py:60
  264.2 5.1 copy-start.5
  264.2 5.1 copy-start.10
  264.8 24.0 %collective-permute-start.3 = (bf16[1,128,1536]{1,2,0:T(8,128)(2,1)S(1)}, bf16[1,128,1536]{1,2,0:T(8,128)(2,1)S(1)}, u32[]{:S(2)}, u32[]{:S(2)}) collective-permute-start(bf16[1,128,1536]{1,2,0:T(8,128)(2,1)S(1)} %get-tuple-element.107), channel_id=1, source_target_pairs={{0,1},{1,2},{2,3},{3,0},{4,5},{5,6},{6,7},{7,4},{8,9},{9,10},{10,1... | collective-permute-start | bytes 1179656 | tf_op jit(solution)/shard_map/ppermute | solution.py:60
  264.9 27.3 %collective-permute-start.4 = (bf16[1,128,1536]{1,2,0:T(8,128)(2,1)S(1)}, bf16[1,128,1536]{1,2,0:T(8,128)(2,1)S(1)}, u32[]{:S(2)}, u32[]{:S(2)}) collective-permute-start(bf16[1,128,1536]{1,2,0:T(8,128)(2,1)S(1)} %get-tuple-element.108), channel_id=1, source_target_pairs={{0,2},{1,3},{2,0},{3,1},{4,6},{5,7},{6,4},{7,5},{8,10},{9,11},{10,... | collective-permute-start | bytes 1179656 | tf_op jit(solution)/shard_map/ppermute | solution.py:60
  269.0 33.5 %collective-permute-start.5 = (bf16[1,128,1536]{1,2,0:T(8,128)(2,1)S(1)}, bf16[1,128,1536]{1,2,0:T(8,128)(2,1)S(1)}, u32[]{:S(2)}, u32[]{:S(2)}) collective-permute-start(bf16[1,128,1536]{1,2,0:T(8,128)(2,1)S(1)} %get-tuple-element.109), channel_id=1, source_target_pairs={{0,3},{1,0},{2,1},{3,2},{4,7},{5,4},{6,5},{7,6},{8,11},{9,8},{10,9... | collective-permute-start | bytes 1179656 | tf_op jit(solution)/shard_map/ppermute | solution.py:60
  270.0 33.0 %copy-start.50 = (bf16[12,64,128]{2,1,0:T(8,128)(2,1)}, bf16[12,64,128]{2,1,0:T(8,128)(2,1)S(1)}, u32[]{:S(2)}) copy-start(bf16[12,64,128]{2,1,0:T(8,128)(2,1)S(1)} %convolution_convert_fusion.14) | copy-start | bytes 589828
  270.0 33.7 %copy-start.37 = (bf16[1,128,768]{2,1,0:T(8,128)(2,1)S(1)}, bf16[1,128,768]{2,1,0:T(8,128)(2,1)}, u32[]{:S(2)}) copy-start(bf16[1,128,768]{2,1,0:T(8,128)(2,1)} %param.21) | copy-start | bytes 589828
  270.0 33.7 %copy-start.58 = (f32[768]{0:T(1024)S(1)}, f32[768]{0:T(1024)}, u32[]{:S(2)}) copy-start(f32[768]{0:T(1024)} %copy-done.57) | copy-start | bytes 9220
  270.0 33.7 %copy-start.68 = (f32[128]{0:T(128)S(1)}, f32[128]{0:T(128)}, u32[]{:S(2)}) copy-start(f32[128]{0:T(128)} %copy-done.67) | copy-start | bytes 1540
  302.9 3.8 copy-start.12
  303.0 3.8 copy-start.28
  303.7 4.6 copy-start.18
  303.7 4.6 copy-start.42
  303.7 4.6 copy-start.53
  303.7 4.6 copy-start.64
  306.7 5.6 %copy-start.15 = (f32[128,768]{1,0:T(8,128)S(1)}, f32[128,768]{1,0:T(8,128)}, u32[]{:S(2)}) copy-start(f32[128,768]{1,0:T(8,128)} %copy-done.13) | copy-start | bytes 1179652
  306.7 5.6 %copy-start.40 = (bf16[12,64,128]{2,1,0:T(8,128)(2,1)S(1)}, bf16[12,64,128]{2,1,0:T(8,128)(2,1)}, u32[]{:S(2)}) copy-start(bf16[12,64,128]{2,1,0:T(8,128)(2,1)} %copy-done.39) | copy-start | bytes 589828
  313.9 5.2 copy-start.48
  313.9 5.2 copy-start.70
  313.9 5.2 copy-start.72
  319.1 6.6 %copy-start.46 = (bf16[128,1536]{0,1:T(8,128)(2,1)S(1)}, bf16[128,1536]{0,1:T(8,128)(2,1)}, u32[]{:S(2)}) copy-start(bf16[128,1536]{0,1:T(8,128)(2,1)} %copy-done.45) | copy-start | bytes 1179652
  325.7 3.6 copy-start.55
  325.8 7.4 %copy-start.26 = (bf16[128,2048]{1,0:T(8,128)(2,1)S(1)}, bf16[128,2048]{1,0:T(8,128)(2,1)}, u32[]{:S(2)}) copy-start(bf16[128,2048]{1,0:T(8,128)(2,1)} %copy-done.25) | copy-start | bytes 1572868
  329.4 1.8 collective-permute-start.9
  331.2 14.2 %copy-start.66 = (f32[128]{0:T(128)S(1)}, f32[128]{0:T(128)}, u32[]{:S(2)}) copy-start(f32[128]{0:T(128)} %get-tuple-element.126) | copy-start | bytes 1540
  331.2 5.0 collective-permute-start.10
  336.3 3.8 collective-permute-start.11
  340.1 4.0 collective-permute-start.12
  344.1 5.7 %collective-permute-start.13 = (f32[21,128]{1,0:T(8,128)S(1)}, f32[21,128]{1,0:T(8,128)S(1)}, u32[]{:S(2)}, u32[]{:S(2)}) collective-permute-start(f32[21,128]{1,0:T(8,128)S(1)} %add.215), channel_id=1, source_target_pairs={{0,16},{4,20},{8,24},{12,28},{16,0},{20,4},{24,8},{28,12},{1,17},{... | collective-permute-start | bytes 32264 | tf_op jit(solution)/shard_map/ppermute | solution.py:84
  (28 other events, 57.4 us)
Sparse Core Ops, SparseCore 0:
  12.3 67.0 all-gather.2
  82.3 104.5 all-gather.4
  230.7 140.3 reduce-scatter.4
  377.8 134.5 reduce-scatter.2
